TPU v7x, 32 devices: a whole 2x2x4 slice. The times are simulated.
32 devices in a mesh: clu: 8 (over y, x, core), mem: 4 (over z).
Axes of the slice: x: 2, y: 2, z: 4, core: 2. Of those that a mesh axis runs over, the one named last changes fastest.
Arguments:
- seed_class: int32 [8192], P(('clu', 'mem')), may hold values from 0 to 15
- seed_weight: float32 [8192], P(('clu', 'mem')), may hold values from 0.3 to 3
- tile_values: bfloat16 [8, 4, 96, 128, 128], P('clu', 'mem'), may hold values from 0 to 1
- tile_rows: int32 [8, 4, 96], P('clu', 'mem'), may hold values from 0 to 7
- tile_cols: int32 [8, 4, 96], P('clu', 'mem'), may hold values from 0 to 15
- tile_count: int32 [8, 4], P('clu', 'mem'), may hold values from 12 to 96, as said below
Outputs:
- scores: float32 [8, 8192], P(None, ('clu', 'mem'))
- residual: float32 [8, 8192], P(None, ('clu', 'mem'))
Inputs may be any that keep to these rules, and one draw needn't show every extreme that they name: `tile_count`: some device uses all 96 slots in every draw.
All inputs are finite; a program needn't handle non-finite values.
Results may differ from a plain program's by a relative error of at most 0.0027.
Values may be sent and summed in bfloat16 or wider, within the bound.
A program may use at most 64 MiB of HBM per device.

v0:
```python
import jax
import jax.numpy as jnp
from jax import lax
from jax.sharding import PartitionSpec as P

CLASSES = 8
NB_DEV = 2
ITERS = 2


def spread(row_part, col_part):
    width = row_part.shape[0]
    from_rows = lax.psum_scatter(
        row_part.reshape(width, -1), "mem", scatter_dimension=1, tiled=True
    )
    from_cols = lax.psum_scatter(
        col_part.reshape(width, -1), "clu", scatter_dimension=1, tiled=True
    )
    return from_rows + from_cols


def squares(residual):
    return lax.psum(jnp.sum(residual * residual, axis=1), ("clu", "mem"))


def on_device(seed_class, seed_weight, tile_values, tile_rows, tile_cols, tile_count):
    tiles = tile_values[0, 0]
    rows = tile_rows[0, 0]
    cols = tile_cols[0, 0]
    count = tile_count[0, 0]
    slots = tiles.shape[0]
    side = tiles.shape[1]
    row_blocks = NB_DEV * lax.axis_size("mem")
    col_blocks = NB_DEV * lax.axis_size("clu")
    valid = (jnp.arange(slots, dtype=jnp.int32) < count).astype(jnp.float32)
    row_table = (rows[None, :] == jnp.arange(row_blocks, dtype=jnp.int32)[:, None]).astype(
        jnp.float32
    ) * valid[None, :]
    col_table = (cols[None, :] == jnp.arange(col_blocks, dtype=jnp.int32)[:, None]).astype(
        jnp.float32
    ) * valid[None, :]
    highest = lax.Precision.HIGHEST
    row_totals = jnp.sum(tiles, axis=2, dtype=jnp.float32)
    col_totals = jnp.sum(tiles, axis=1, dtype=jnp.float32)
    row_part = jnp.einsum("rt,ti->ri", row_table, row_totals, precision=highest)
    col_part = jnp.einsum("kt,tj->kj", col_table, col_totals, precision=highest)
    degree = 1.0 + spread(row_part[None], col_part[None])[0]
    inverse_root = lax.rsqrt(degree)
    classes_now = jnp.arange(CLASSES, dtype=jnp.int32)[:, None]
    labels = jnp.where(seed_class[None, :] == classes_now, seed_weight[None, :], jnp.float32(0.0))
    scores = jnp.zeros_like(labels)
    residual = labels
    direction = labels
    norm_now = squares(residual)
    for step in range(ITERS):
        width = direction.shape[0]
        scaled = (inverse_root[None, :] * direction).astype(jnp.bfloat16)
        col_panel = lax.all_gather(scaled, "clu", axis=1, tiled=True).reshape(
            width, col_blocks, side
        )
        row_panel = lax.all_gather(scaled, "mem", axis=1, tiled=True).reshape(
            width, row_blocks, side
        )
        forward = jnp.einsum(
            "tij,ctj->cti",
            tiles,
            jnp.take(col_panel, cols, axis=1),
            preferred_element_type=jnp.float32,
        )
        backward = jnp.einsum(
            "tij,cti->ctj",
            tiles,
            jnp.take(row_panel, rows, axis=1),
            preferred_element_type=jnp.float32,
        )
        row_sum = jnp.einsum("rt,cti->cri", row_table, forward, precision=highest)
        col_sum = jnp.einsum("kt,ctj->ckj", col_table, backward, precision=highest)
        image_sum = spread(row_sum, col_sum)
        image = direction - 0.99 * inverse_root[None, :] * image_sum
        alpha = norm_now / lax.psum(jnp.sum(direction * image, axis=1), ("clu", "mem"))
        scores = scores + alpha[:, None] * direction
        residual = residual - alpha[:, None] * image
        if step + 1 < ITERS:
            norm_next = squares(residual)
            direction = residual + (norm_next / norm_now)[:, None] * direction
            norm_now = norm_next
    return (scores, residual)


def solution(mesh):
    in_specs = (
        P(("clu", "mem")),
        P(("clu", "mem")),
        P("clu", "mem", None, None, None),
        P("clu", "mem", None),
        P("clu", "mem", None),
        P("clu", "mem"),
    )
    out_specs = (P(None, ("clu", "mem")), P(None, ("clu", "mem")))
    return jax.shard_map(
        on_device, mesh=mesh, in_specs=in_specs, out_specs=out_specs, check_vma=False
    )
```

profile of v0, /device:TPU:0, one launch (start us, length us, event | category | flops | bytes accessed | tf_op | source)
XLA Modules:
  0.0 363.4 jit_solution(1436523497053478819)
XLA Ops:
  7.2 0.0 reduce-scatter.19.cloned.1.call-start
  7.3 3.0 convert_reduce_fusion
  10.9 0.1 fusion.39
  11.1 1.1 copy.12
  12.1 0.0 reduce-scatter.19.cloned.1.call-update
  12.2 0.0 reduce-scatter.21.cloned.1.call-start
  12.2 0.1 fusion.32
  12.4 1.4 copy.14
  13.8 0.0 reduce-scatter.11.cloned.1.call-start
  13.9 22.8 %reduce-scatter.19.cloned.1.call-done = f32[256,1]{1,0:T(8,128)} async-done(((f32[1024,1]{1,0:T(8,128)}), f32[256,1]{1,0:T(8,128)}) %reduce-scatter.19.cloned.1.call-update) | async-done | bytes 1040
  36.7 1.0 copy.13
  37.7 36.6 %reduce-scatter.21.cloned.1.call-done = f32[256,1]{1,0:T(8,128)} async-done(((f32[2048,1]{1,0:T(8,128)}), f32[256,1]{1,0:T(8,128)}) %reduce-scatter.21.cloned.1.call-update) | async-done | bytes 1040
  74.2 1.0 copy.15
  75.3 9.0 %all_gather.12 = bf16[8,2048]{1,0:T(8,128)(2,1)S(1)} all-gather(bf16[8,256]{1,0:T(8,128)(2,1)S(1)} %fusion.35), channel_id=1, replica_groups=mesh['clu'=8,'mem'=4] {'clu'}, dimensions={1}, use_global_device_ids=true | all-gather | bytes 36864 | tf_op jit(solution)/shard_map/all_gather | solution.py:58
  84.2 13.2 %all_gather.13 = bf16[8,1024]{1,0:T(8,128)(2,1)S(1)} all-gather(bf16[8,256]{1,0:T(8,128)(2,1)S(1)} %fusion.35), channel_id=1, replica_groups=mesh['clu'=8,'mem'=4] {'mem'}, dimensions={1}, use_global_device_ids=true | all-gather | bytes 20480 | tf_op jit(solution)/shard_map/all_gather | solution.py:61
  97.4 0.7 gather_fusion
  98.1 1.7 fusion.6
  99.8 0.4 convolution_bitcast_fusion.3
  100.2 0.6 copy.43
  100.9 0.0 reduce-scatter.13.cloned.1.call-start
  100.9 0.7 gather_fusion.1
  101.6 1.0 fusion.4
  102.6 0.4 convolution_bitcast_fusion.1
  102.9 0.6 copy.41
  103.6 0.0 reduce-scatter.15.cloned.1.call-start
  103.6 16.2 %reduce-scatter.11.cloned.1.call-done = f32[8,256]{1,0:T(8,128)} async-done(((f32[8,1024]{1,0:T(8,128)}), f32[8,256]{1,0:T(8,128)}) %reduce-scatter.11.cloned.1.call-update) | async-done | bytes 8208 | tf_op jit(solution)/shard_map/reduce_scatter | solution.py:13
  119.9 34.5 %reduce-scatter.13.cloned.1.call-done = f32[8,256]{1,0:T(8,128)} async-done(((f32[8,2048]{1,0:T(8,128)}), f32[8,256]{1,0:T(8,128)}) %reduce-scatter.13.cloned.1.call-update) | async-done | bytes 8208 | tf_op jit(solution)/shard_map/reduce_scatter | solution.py:16
  154.4 0.9 fusion.36
  155.3 39.4 %all-reduce = (f32[8]{0:T(128)S(1)}, f32[8]{0:T(128)S(1)}) all-reduce(f32[8]{0:T(128)S(1)} %get-tuple-element.7, f32[8]{0:T(128)S(1)} %get-tuple-element.6), channel_id=1, replica_groups=mesh['clu'=8,'mem'=4] {'clu','mem'}, use_global_device_ids=true, to_apply=%region_1.0 | all-reduce | flops 16 | bytes 128 | tf_op jit(solution)/shard_map/psum | solution.py:23
  194.7 0.2 multiply_reduce_fusion.1
  194.8 41.0 %psum.30 = f32[8]{0:T(128)S(1)} all-reduce(f32[8]{0:T(128)S(1)} %multiply_reduce_fusion.1), channel_id=1, replica_groups=mesh['clu'=8,'mem'=4] {'clu','mem'}, use_global_device_ids=true, to_apply=%region_11.14 | all-reduce | flops 8 | bytes 64 | tf_op jit(solution)/shard_map/psum | solution.py:23
  235.9 0.1 multiply_convert_fusion
  235.9 9.8 %all_gather.14 = bf16[8,2048]{1,0:T(8,128)(2,1)S(1)} all-gather(bf16[8,256]{1,0:T(8,128)(2,1)S(1)} %multiply_convert_fusion), channel_id=1, replica_groups=mesh['clu'=8,'mem'=4] {'clu'}, dimensions={1}, use_global_device_ids=true | all-gather | bytes 36864 | tf_op jit(solution)/shard_map/all_gather | solution.py:58
  245.8 13.1 %all_gather.15 = bf16[8,1024]{1,0:T(8,128)(2,1)S(1)} all-gather(bf16[8,256]{1,0:T(8,128)(2,1)S(1)} %multiply_convert_fusion), channel_id=1, replica_groups=mesh['clu'=8,'mem'=4] {'mem'}, dimensions={1}, use_global_device_ids=true | all-gather | bytes 20480 | tf_op jit(solution)/shard_map/all_gather | solution.py:61
  258.9 0.7 gather_fusion.2
  259.5 1.7 fusion.2
  261.3 0.4 convolution_bitcast_fusion.2
  261.7 0.6 copy.42
  262.3 0.0 reduce-scatter.17.cloned.1.call-start
  262.4 0.7 gather_fusion.3
  263.0 1.0 fusion
  264.0 0.4 convolution_bitcast_fusion
  264.4 0.6 copy.40
  265.0 15.3 %reduce-scatter.15.cloned.1.call-done = f32[8,256]{1,0:T(8,128)} async-done(((f32[8,1024]{1,0:T(8,128)}), f32[8,256]{1,0:T(8,128)}) %reduce-scatter.15.cloned.1.call-update) | async-done | bytes 8208 | tf_op jit(solution)/shard_map/reduce_scatter | solution.py:13
  280.4 34.5 %reduce-scatter.17.cloned.1.call-done = f32[8,256]{1,0:T(8,128)} async-done(((f32[8,2048]{1,0:T(8,128)}), f32[8,256]{1,0:T(8,128)}) %reduce-scatter.17.cloned.1.call-update) | async-done | bytes 8208 | tf_op jit(solution)/shard_map/reduce_scatter | solution.py:16
  314.9 0.9 multiply_reduce_fusion
  315.8 39.3 %psum.31 = f32[8]{0:T(128)S(1)} all-reduce(f32[8]{0:T(128)S(1)} %multiply_reduce_fusion), channel_id=1, replica_groups=mesh['clu'=8,'mem'=4] {'clu','mem'}, use_global_device_ids=true, to_apply=%region_15.18 | all-reduce | flops 8 | bytes 64 | tf_op jit(solution)/shard_map/psum | solution.py:80
  355.1 1.4 multiply_subtract_fusion
  (27 shorter events, 0.2 us)
Async XLA Ops:
  7.2 90.9 %copy-start = (bf16[1,1,96,128,128]{4,3,2,1,0:T(8,128)(2,1)S(1)}, bf16[1,1,96,128,128]{4,3,2,1,0:T(8,128)(2,1)}, u32[]{:S(2)}) copy-start(bf16[1,1,96,128,128]{4,3,2,1,0:T(8,128)(2,1)} %param.12) | copy-start | bytes 9437188
  7.2 3.7 %copy-start.3 = (s32[1,1,96]{2,1,0:T(1,128)S(1)}, s32[1,1,96]{2,1,0:T(1,128)}, u32[]{:S(2)}) copy-start(s32[1,1,96]{2,1,0:T(1,128)} %param.13) | copy-start | bytes 1156
  7.2 5.0 %copy-start.4 = (s32[1,1,96]{2,1,0:T(1,128)S(1)}, s32[1,1,96]{2,1,0:T(1,128)}, u32[]{:S(2)}) copy-start(s32[1,1,96]{2,1,0:T(1,128)} %param.14) | copy-start | bytes 1156
  7.2 68.0 %copy-start.1 = (f32[256]{0:T(256)S(1)}, f32[256]{0:T(256)}, u32[]{:S(2)}) copy-start(f32[256]{0:T(256)} %param.11) | copy-start | bytes 3076
  7.2 68.0 %copy-start.2 = (s32[256]{0:T(256)S(1)}, s32[256]{0:T(256)}, u32[]{:S(2)}) copy-start(s32[256]{0:T(256)} %param.10) | copy-start | bytes 3076
  7.2 29.5 %reduce-scatter.19.cloned.1.call-start = ((), (), s32[]{:S(2)}) async-start(), calls=%async_computation.10 | async-start | bytes 655360
  12.2 62.1 %reduce-scatter.21.cloned.1.call-start = ((), (), s32[]{:S(2)}) async-start(), calls=%async_computation.11 | async-start | bytes 1179648
  13.8 106.1 %reduce-scatter.11.cloned.1.call-start = ((), (), s32[]{:S(2)}) async-start(), calls=%async_computation.6 | async-start | bytes 40960 | tf_op jit(solution)/shard_map/reduce_scatter | solution.py:13
  100.9 53.6 %reduce-scatter.13.cloned.1.call-start = ((), (), s32[]{:S(2)}) async-start(), calls=%async_computation.7 | async-start | bytes 73728 | tf_op jit(solution)/shard_map/reduce_scatter | solution.py:16
  103.6 176.8 %reduce-scatter.15.cloned.1.call-start = ((), (), s32[]{:S(2)}) async-start(), calls=%async_computation.8 | async-start | bytes 40960 | tf_op jit(solution)/shard_map/reduce_scatter | solution.py:13
  262.3 52.6 %reduce-scatter.17.cloned.1.call-start = ((), (), s32[]{:S(2)}) async-start(), calls=%async_computation.9 | async-start | bytes 73728 | tf_op jit(solution)/shard_map/reduce_scatter | solution.py:16
Sparse Core Ops, SparseCore 0:
  12.3 24.3 reduce-scatter.18
  39.9 34.3 reduce-scatter.20
  101.0 18.8 reduce-scatter.10
  123.0 31.3 reduce-scatter.12
  262.4 17.8 reduce-scatter.14
  283.5 31.3 reduce-scatter.16
where the time goes:
time: 364 us; the launch traced here: 363 us
  blocking collectives  165 us (45%)
  waiting for transfers between devices  160 us (44%)
  between operations  14.9 us (4%)
  local copies, waits for them, and re-layouts  9.59 us (3%)
  matrix products  7.24 us (2%)
  other arithmetic  6.48 us (2%)
    psum x2, blocking collectives, squares(): return lax.psum(jnp.sum(residual * residual, axis=1), ('clu', 'mem'))  80.4 us
    reduce_scatter x2, waiting for transfers between devices, spread(): lax.psum_scatter(col_part.reshape(width, -1), 'clu', scatter_dimension=1,...  69.1 us
    unnamed x8, waiting for transfers between devices  59.5 us
    psum x1, blocking collectives, on_device(): lax.psum(jnp.sum(direction * image, axis=1), ('clu', 'mem'))  39.3 us
    reduce_scatter x2, waiting for transfers between devices, spread(): lax.psum_scatter(row_part.reshape(width, -1), 'mem', scatter_dimension=1,...  31.6 us
    all_gather x2, blocking collectives, on_device(): lax.all_gather(scaled, 'mem', axis=1, tiled=True)  26.3 us
    all_gather x2, blocking collectives, on_device(): lax.all_gather(scaled, 'clu', axis=1, tiled=True)  18.8 us
  transfers between devices with their start and end apart: 6, of which 6 were waited for; matrix products, arithmetic and copies ran while one was open for 2% of the time, Pallas kernels for 0%

commit v1 on v0

--- a/solution.py
+++ b/solution.py
@@ -1,11 +1,17 @@
+import functools
 import jax
 import jax.numpy as jnp
 from jax import lax
+from jax.experimental import pallas as pl
+from jax.experimental.pallas import tpu as pltpu
 from jax.sharding import PartitionSpec as P
 
 CLASSES = 8
 NB_DEV = 2
 ITERS = 2
+CHUNKS = 4
+DENSE_LIMIT = 16 * 1024 * 1024
+MESH = pl.DeviceIdType.MESH
 
 
 def spread(row_part, col_part):
@@ -23,7 +29,7 @@
     return lax.psum(jnp.sum(residual * residual, axis=1), ("clu", "mem"))
 
 
-def on_device(seed_class, seed_weight, tile_values, tile_rows, tile_cols, tile_count):
+def on_device_slots(seed_class, seed_weight, tile_values, tile_rows, tile_cols, tile_count):
     tiles = tile_values[0, 0]
     rows = tile_rows[0, 0]
     cols = tile_cols[0, 0]
@@ -87,6 +93,353 @@
     return (scores, residual)
 
 
+def densify_kernel(
+    rows_ref, cols_ref, count_ref, tiles_hbm, w_ref, row_ref, col_ref, tiles, dense, sems
+):
+    slots, side, _ = tiles.shape
+    row_blocks = w_ref.shape[0] // side
+    col_blocks = w_ref.shape[1] // side
+    chunk = slots // CHUNKS
+    copies = [
+        pltpu.make_async_copy(
+            tiles_hbm.at[pl.ds(k * chunk, chunk)], tiles.at[pl.ds(k * chunk, chunk)], sems.at[k]
+        )
+        for k in range(CHUNKS)
+    ]
+    for copy in copies:
+        copy.start()
+
+    def clear(k, carry):
+        dense[k] = jnp.zeros((side, side), jnp.float32)
+        return carry
+
+    lax.fori_loop(0, row_blocks * col_blocks, clear, 0)
+    count = count_ref[0]
+
+    def add(s, carry):
+        place = rows_ref[s] * col_blocks + cols_ref[s]
+        dense[place] += tiles[s].astype(jnp.float32)
+        return carry
+
+    for k in range(CHUNKS):
+        copies[k].wait()
+        lax.fori_loop(k * chunk, jnp.clip(count, k * chunk, (k + 1) * chunk), add, 0)
+
+    col_sums = [jnp.zeros((8, side), jnp.float32) for _ in range(col_blocks)]
+    for r in range(row_blocks):
+        row_sum = jnp.zeros((side, side), jnp.float32)
+        for c in range(col_blocks):
+            block = dense[r * col_blocks + c]
+            w_ref[r * side : (r + 1) * side, c * side : (c + 1) * side] = block.astype(jnp.bfloat16)
+            row_sum = row_sum + block
+            col_sums[c] = col_sums[c] + jnp.sum(block.reshape(side // 8, 8, side), axis=0)
+        at = (r % NB_DEV) * side
+        row_ref[r // NB_DEV, :, at : at + side] = jnp.sum(row_sum.T, axis=0, keepdims=True)
+    for c in range(col_blocks):
+        at = (c % NB_DEV) * side
+        col_ref[c // NB_DEV, :, at : at + side] = jnp.sum(col_sums[c], axis=0, keepdims=True)
+
+
+def split(panel):
+    high = panel.astype(jnp.bfloat16)
+    low = (panel - high.astype(jnp.float32)).astype(jnp.bfloat16)
+    return jnp.concatenate([high, low], axis=0)
+
+
+def solve_kernel(
+    n_clu,
+    n_mem,
+    class_ref,
+    weight_ref,
+    w_hbm,
+    row_ref,
+    col_ref,
+    scores_ref,
+    residual_ref,
+    w,
+    deg_m,
+    deg_c,
+    own,
+    pan_m,
+    pan_c,
+    part_m,
+    part_c,
+    got_m,
+    got_c,
+    dots,
+    got_dots,
+    w_sem,
+    send_m,
+    recv_m,
+    send_c,
+    recv_c,
+    send_d,
+    recv_d,
+):
+    me_c = lax.axis_index("clu")
+    me_m = lax.axis_index("mem")
+    total = n_clu * n_mem
+    place = me_c * n_mem + me_m
+
+    def member(k):
+        other = lax.rem(place + k, total)
+        return (lax.div(other, n_mem), lax.rem(other, n_mem))
+
+    w_copy = pltpu.make_async_copy(w_hbm, w, w_sem)
+    w_copy.start()
+    barrier = pltpu.get_barrier_semaphore()
+
+    def greet(k, carry):
+        pl.semaphore_signal(barrier, inc=1, device_id=member(k), device_id_type=MESH)
+        return carry
+
+    lax.fori_loop(1, total, greet, 0)
+
+    sent = []
+
+    def over_mem(phase, source, target):
+        copies = []
+        for k in range(1, n_mem):
+            other = lax.rem(me_m + k, n_mem)
+            copies.append(
+                pltpu.make_async_remote_copy(
+                    src_ref=source(other),
+                    dst_ref=target(k),
+                    send_sem=send_m.at[phase, k],
+                    recv_sem=recv_m.at[phase, k],
+                    device_id=(me_c, other),
+                    device_id_type=MESH,
+                )
+            )
+            copies[-1].start()
+        sent.extend(copies)
+        return copies
+
+    def over_clu(phase, source, target):
+        copies = []
+        for k in range(1, n_clu):
+            other = lax.rem(me_c + k, n_clu)
+            copies.append(
+                pltpu.make_async_remote_copy(
+                    src_ref=source(other),
+                    dst_ref=target(k),
+                    send_sem=send_c.at[phase, k],
+                    recv_sem=recv_c.at[phase, k],
+                    device_id=(other, me_m),
+                    device_id_type=MESH,
+                )
+            )
+            copies[-1].start()
+        sent.extend(copies)
+        return copies
+
+    def arrive(copies):
+        for copy in copies:
+            copy.wait_recv()
+
+    weight = weight_ref[...]
+    kinds = lax.broadcasted_iota(jnp.int32, (CLASSES, weight.shape[1]), 0)
+    labels = jnp.where(class_ref[...] == kinds, weight, jnp.float32(0.0))
+    pl.semaphore_wait(barrier, total - 1)
+
+    from_m = over_mem(0, lambda o: row_ref.at[o], lambda k: deg_m.at[k])
+    from_c = over_clu(0, lambda o: col_ref.at[o], lambda k: deg_c.at[k])
+    degree = 1.0 + (row_ref[me_m] + col_ref[me_c])
+    arrive(from_m)
+    for k in range(1, n_mem):
+        degree = degree + deg_m[k]
+    arrive(from_c)
+    for k in range(1, n_clu):
+        degree = degree + deg_c[k]
+    root = lax.rsqrt(degree)
+
+    def gather(step, panel):
+        own[step] = panel
+        pan_m[step, me_m] = panel
+        pan_c[step, me_c] = panel
+        from_m = over_mem(1 + 2 * step, lambda o: own.at[step], lambda k: pan_m.at[step, me_m])
+        from_c = over_clu(1 + 2 * step, lambda o: own.at[step], lambda k: pan_c.at[step, me_c])
+        return from_m, from_c
+
+    def multiply(step, from_m, from_c, prepare):
+        phase = 2 + 2 * step
+        arrive(from_m)
+        left = jnp.concatenate([pan_m[step, k] for k in range(n_mem)], axis=1)
+        if step == 0:
+            w_copy.wait()
+        out = lax.dot_general(
+            prepare(left), w[...], (((1,), (0,)), ((), ())), preferred_element_type=jnp.float32
+        )
+        out = out[:CLASSES] if step == 0 else out[:CLASSES] + out[CLASSES:]
+        width = out.shape[1] // n_clu
+        for k in range(n_clu):
+            part_c[step, k] = out[:, k * width : (k + 1) * width]
+        back_c = over_clu(phase, lambda o: part_c.at[step, o], lambda k: got_c.at[step, k])
+        arrive(from_c)
+        right = jnp.concatenate([pan_c[step, k] for k in range(n_clu)], axis=1)
+        out = lax.dot_general(
+            prepare(right), w[...], (((1,), (1,)), ((), ())), preferred_element_type=jnp.float32
+        )
+        out = out[:CLASSES] if step == 0 else out[:CLASSES] + out[CLASSES:]
+        for k in range(n_mem):
+            part_m[step, k] = out[:, k * width : (k + 1) * width]
+        back_m = over_mem(phase, lambda o: part_m.at[step, o], lambda k: got_m.at[step, k])
+        return back_m, back_c, jnp.sum(left * out, axis=1, keepdims=True)
+
+    def collect(step, back_m, back_c):
+        image = part_m[step, me_m] + part_c[step, me_c]
+        arrive(back_c)
+        for k in range(1, n_clu):
+            image = image + got_c[step, k]
+        arrive(back_m)
+        for k in range(1, n_mem):
+            image = image + got_m[step, k]
+        return 0.99 * root * image
+
+    from_m, from_c = gather(0, root * labels)
+    back_m, back_c, _ = multiply(0, from_m, from_c, lambda x: x.astype(jnp.bfloat16))
+    first = collect(0, back_m, back_c)
+
+    from_m, from_c = gather(1, root * first)
+    sums = [
+        jnp.sum(labels * labels, axis=1, keepdims=True),
+        jnp.sum(labels * first, axis=1, keepdims=True),
+        jnp.sum(first * first, axis=1, keepdims=True),
+    ]
+    back_m, back_c, cross = multiply(1, from_m, from_c, split)
+    sums.append(1.98 * cross)
+
+    lane = lax.broadcasted_iota(jnp.int32, (CLASSES, 128), 1)
+    kind = lax.broadcasted_iota(jnp.int32, (CLASSES, 128), 0)
+    line = jnp.zeros((CLASSES, 128), jnp.float32)
+    for k, value in enumerate(sums):
+        line = line + jnp.where(lane == kind + k * CLASSES, value, 0.0)
+    line = jnp.sum(line, axis=0, keepdims=True)
+    dots[...] = line
+
+    def dot_copy(k):
+        return pltpu.make_async_remote_copy(
+            src_ref=dots,
+            dst_ref=got_dots.at[k],
+            send_sem=send_d.at[k],
+            recv_sem=recv_d.at[k],
+            device_id=member(k),
+            device_id_type=MESH,
+        )
+
+    def send_dot(k, carry):
+        dot_copy(k).start()
+        return carry
+
+    def take_dot(k, carry):
+        dot_copy(k).wait_recv()
+        return carry + got_dots[k]
+
+    lax.fori_loop(1, total, send_dot, 0)
+    second = collect(1, back_m, back_c)
+    line = lax.fori_loop(1, total, take_dot, line)
+    spread_line = jnp.broadcast_to(line, (CLASSES, 128))
+    bb, bq, qq, qt = [
+        jnp.sum(
+            jnp.where(lane == kind + k * CLASSES, spread_line, 0.0), axis=1, keepdims=True
+        )
+        for k in range(4)
+    ]
+    alpha = bb / (bb - bq)
+    ratio = bq / bb
+    norm = alpha * alpha * (qq - ratio * bq)
+    beta = norm / bb
+    h = beta - alpha * ratio
+    curve = alpha * alpha * (qq - qt) + 2.0 * alpha * h * (bq - qq) + h * h * (bb - bq)
+    alpha_next = norm / curve
+    direction = alpha * first + h * labels
+    image = alpha * (first - second) + h * (labels - first)
+    scores_ref[...] = alpha * labels + alpha_next * direction
+    residual_ref[...] = alpha * (first - ratio * labels) - alpha_next * image
+
+    def leave_dot(k, carry):
+        dot_copy(k).wait_send()
+        return carry
+
+    lax.fori_loop(1, total, leave_dot, 0)
+    for copy in sent:
+        copy.wait_send()
+
+
+def on_device_dense(seed_class, seed_weight, tile_values, tile_rows, tile_cols, tile_count):
+    n_clu = lax.axis_size("clu")
+    n_mem = lax.axis_size("mem")
+    tiles = tile_values[0, 0]
+    slots, side, _ = tiles.shape
+    nodes = NB_DEV * side
+    rows = nodes * n_mem
+    cols = nodes * n_clu
+    f32 = jnp.float32
+    smem = pl.BlockSpec(memory_space=pltpu.SMEM)
+    vmem = pl.BlockSpec(memory_space=pltpu.VMEM)
+    hbm = pl.BlockSpec(memory_space=pl.ANY)
+    w, row_total, col_total = pl.pallas_call(
+        densify_kernel,
+        out_shape=(
+            jax.ShapeDtypeStruct((rows, cols), jnp.bfloat16),
+            jax.ShapeDtypeStruct((n_mem, 1, nodes), f32),
+            jax.ShapeDtypeStruct((n_clu, 1, nodes), f32),
+        ),
+        in_specs=[smem, smem, smem, hbm],
+        out_specs=(vmem, vmem, vmem),
+        scratch_shapes=[
+            pltpu.VMEM((slots, side, side), tiles.dtype),
+            pltpu.VMEM((rows * cols // (side * side), side, side), f32),
+            pltpu.SemaphoreType.DMA((CHUNKS,)),
+        ],
+        compiler_params=pltpu.CompilerParams(vmem_limit_bytes=24 * 1024 * 1024),
+        name="densify",
+    )(tile_rows[0, 0], tile_cols[0, 0], tile_count[0], tiles)
+    panel = (CLASSES, nodes)
+    dma = pltpu.SemaphoreType.DMA
+    return pl.pallas_call(
+        functools.partial(solve_kernel, n_clu, n_mem),
+        out_shape=(jax.ShapeDtypeStruct(panel, f32), jax.ShapeDtypeStruct(panel, f32)),
+        in_specs=[vmem, vmem, hbm, vmem, vmem],
+        out_specs=(vmem, vmem),
+        scratch_shapes=[
+            pltpu.VMEM((rows, cols), jnp.bfloat16),
+            pltpu.VMEM((n_mem, 1, nodes), f32),
+            pltpu.VMEM((n_clu, 1, nodes), f32),
+            pltpu.VMEM((ITERS, *panel), f32),
+            pltpu.VMEM((ITERS, n_mem, *panel), f32),
+            pltpu.VMEM((ITERS, n_clu, *panel), f32),
+            pltpu.VMEM((ITERS, n_mem, *panel), f32),
+            pltpu.VMEM((ITERS, n_clu, *panel), f32),
+            pltpu.VMEM((ITERS, n_mem, *panel), f32),
+            pltpu.VMEM((ITERS, n_clu, *panel), f32),
+            pltpu.VMEM((1, 128), f32),
+            pltpu.VMEM((n_clu * n_mem, 1, 128), f32),
+            dma,
+            dma((1 + 2 * ITERS, n_mem)),
+            dma((1 + 2 * ITERS, n_mem)),
+            dma((1 + 2 * ITERS, n_clu)),
+            dma((1 + 2 * ITERS, n_clu)),
+            dma((n_clu * n_mem,)),
+            dma((n_clu * n_mem,)),
+        ],
+        compiler_params=pltpu.CompilerParams(
+            collective_id=0, has_side_effects=True, vmem_limit_bytes=16 * 1024 * 1024
+        ),
+        name="solve",
+    )(seed_class[None], seed_weight[None], w, row_total, col_total)
+
+
+def on_device(seed_class, seed_weight, tile_values, tile_rows, tile_cols, tile_count):
+    side = tile_values.shape[-1]
+    blocks = NB_DEV * lax.axis_size("mem") * NB_DEV * lax.axis_size("clu")
+    if blocks * side * side * 4 <= DENSE_LIMIT:
+        run = on_device_dense
+    else:
+        run = on_device_slots
+    return run(seed_class, seed_weight, tile_values, tile_rows, tile_cols, tile_count)
+
+
 def solution(mesh):
     in_specs = (
         P(("clu", "mem")),

time: 364 us -> 42.6 us (0.12)
  blocking collectives: 165 us -> 0 us
  waiting for transfers between devices: 160 us -> 0 us
  Pallas kernels: 0 us -> 35.2 us
  between operations: 14.9 us -> 1.31 us
  matrix products: 7.24 us -> 0 us
  other arithmetic: 6.48 us -> 0 us
  local copies, waits for them, and re-layouts: 9.59 us -> 5.74 us
    psum x3 -> x0, blocking collectives: 120 us -> none  [the longest x2 80.4 us: squares(): return lax.psum(jnp.sum(residual * residual, axis=1), ('clu', 'mem'))]
    reduce_scatter x4 -> x0, waiting for transfers between devices: 101 us -> none  [the longest x2 69.1 us: spread(): lax.psum_scatter(col_part.reshape(width, -1), 'clu', scatter_dimension=1,...]
    unnamed x8 -> x0, waiting for transfers between devices: 59.5 us -> none
    all_gather x4 -> x0, blocking collectives: 45.1 us -> none  [the longest x2 26.3 us: on_device(): lax.all_gather(scaled, 'mem', axis=1, tiled=True)]
    pallas_call x0 -> x2, Pallas kernels: none -> 35.2 us  [the longest x1 32 us: on_device_dense(): pl.pallas_call(functools.partial(solve_kernel, n_clu, n_mem), out_shape=(...]
    dot_general x10 -> x0, matrix products: 7.24 us -> none  [the longest x2 3.49 us: on_device(): jnp.einsum('tij,ctj->cti', tiles, jnp.take(col_panel, cols, axis=1), pref...]
    reduce_sum x4 -> x0, other arithmetic: 4.93 us -> none  [the longest x1 2.99 us: on_device(): col_totals = jnp.sum(tiles, axis=1, dtype=jnp.float32)]
  transfers between devices with their start and end apart: 6 -> 0, of which waited for: 6 -> 0; matrix products, arithmetic and copies ran while one was open for 2% -> 0% of each run, Pallas kernels for 0% -> 0%
where the time goes in v1:
time: 42.6 us; the launch traced here: 42.2 us
  Pallas kernels  35.2 us (83%)
  local copies, waits for them, and re-layouts  5.74 us (13%)
  between operations  1.31 us (3%)
    pallas_call x1, Pallas kernels, on_device_dense(): pl.pallas_call(functools.partial(solve_kernel, n_clu, n_mem), out_shape=(...  32 us
    unnamed x12, local copies, waits for them, and re-layouts  5.74 us
    pallas_call x1, Pallas kernels, on_device_dense(): pl.pallas_call(densify_kernel, out_shape=(jax.ShapeDtypeStruct((rows, col...  3.15 us

profile of v1, /device:TPU:0, one launch (start us, length us, event | category | flops | bytes accessed | tf_op | source)
XLA Modules:
  0.0 42.2 jit_solution(9281874635651382999)
XLA Ops:
  1.3 0.0 copy-start
  1.3 1.9 %copy-done = bf16[1,1,96,128,128]{4,3,2,1,0:T(8,128)(2,1)S(1)} copy-done((bf16[1,1,96,128,128]{4,3,2,1,0:T(8,128)(2,1)S(1)}, bf16[1,1,96,128,128]{4,3,2,1,0:T(8,128)(2,1)}, u32[]{:S(2)}) %copy-start) | copy-done | bytes 3145752
  3.2 0.0 copy-start.3
  3.2 0.7 %copy-done.3 = s32[1,1,96]{2,1,0:T(1,128)S(1)} copy-done((s32[1,1,96]{2,1,0:T(1,128)S(1)}, s32[1,1,96]{2,1,0:T(1,128)}, u32[]{:S(2)}) %copy-start.3) | copy-done | bytes 408
  3.8 0.0 copy-start.4
  3.8 0.7 %copy-done.4 = s32[1,1,96]{2,1,0:T(1,128)S(1)} copy-done((s32[1,1,96]{2,1,0:T(1,128)S(1)}, s32[1,1,96]{2,1,0:T(1,128)}, u32[]{:S(2)}) %copy-start.4) | copy-done | bytes 408
  4.5 3.1 %densify.1 = (bf16[1024,2048]{1,0:T(8,128)(2,1)S(1)}, f32[4,1,256]{2,1,0:T(1,128)S(1)}, f32[8,1,256]{2,1,0:T(1,128)S(1)}) custom-call(s32[96]{0:T(128)S(1)} %bitcast.10, s32[96]{0:T(128)S(1)} %bitcast.11, s32[1]{0:T(128)} %bitcast.6.count_ref, bf16[96,128,128]{2,1,0:T(8,128)(2,1)S(1)} %bitcast.7), custom_call_target="tpu_custom_call" | custom-call | tf_op jit(solution)/shard_map/densify/pallas_call | solution.py:381
  7.6 0.0 copy-start.1
  7.6 0.7 %copy-done.1 = s32[256]{0:T(256)S(1)} copy-done((s32[256]{0:T(256)S(1)}, s32[256]{0:T(256)}, u32[]{:S(2)}) %copy-start.1) | copy-done | bytes 1048
  8.3 0.0 copy-start.2
  8.3 0.7 %copy-done.2 = f32[256]{0:T(256)S(1)} copy-done((f32[256]{0:T(256)S(1)}, f32[256]{0:T(256)}, u32[]{:S(2)}) %copy-start.2) | copy-done | bytes 1048
  9.0 32.0 %solve.1 = (f32[8,256]{1,0:T(8,128)S(1)}, f32[8,256]{1,0:T(8,128)S(1)}) custom-call(s32[1,256]{1,0:T(1,128)S(1)} %bitcast.8, f32[1,256]{1,0:T(1,128)S(1)} %bitcast.9, bf16[1024,2048]{1,0:T(8,128)(2,1)S(1)} %get-tuple-element.5.w_hbm, f32[4,1,256]{2,1,0:T(1,128)S(1)} %get-tuple-element.6.row_ref, f32[8,1,256]{2,1,0:T(1,128)S(1)} %get-tuple-element.7.col_ref), custom_call_target="tpu_custom_call" | custom-call | tf_op jit(solution)/shard_map/solve/pallas_call | solution.py:400
  41.0 0.6 %copy.11 = f32[8,256]{1,0:T(8,128)} copy(f32[8,256]{1,0:T(8,128)S(1)} %get-tuple-element.10) | data formatting | bytes 16384
  41.6 0.6 %copy.12 = f32[8,256]{1,0:T(8,128)} copy(f32[8,256]{1,0:T(8,128)S(1)} %get-tuple-element.11) | data formatting | bytes 16384
Async XLA Ops:
  1.3 1.9 %copy-start = (bf16[1,1,96,128,128]{4,3,2,1,0:T(8,128)(2,1)S(1)}, bf16[1,1,96,128,128]{4,3,2,1,0:T(8,128)(2,1)}, u32[]{:S(2)}) copy-start(bf16[1,1,96,128,128]{4,3,2,1,0:T(8,128)(2,1)} %param.8) | copy-start | bytes 9437188
  3.2 0.7 %copy-start.3 = (s32[1,1,96]{2,1,0:T(1,128)S(1)}, s32[1,1,96]{2,1,0:T(1,128)}, u32[]{:S(2)}) copy-start(s32[1,1,96]{2,1,0:T(1,128)} %param.9) | copy-start | bytes 1156
  3.8 0.7 %copy-start.4 = (s32[1,1,96]{2,1,0:T(1,128)S(1)}, s32[1,1,96]{2,1,0:T(1,128)}, u32[]{:S(2)}) copy-start(s32[1,1,96]{2,1,0:T(1,128)} %param.10) | copy-start | bytes 1156
  7.6 0.7 %copy-start.1 = (s32[256]{0:T(256)S(1)}, s32[256]{0:T(256)}, u32[]{:S(2)}) copy-start(s32[256]{0:T(256)} %param.6) | copy-start | bytes 3076
  8.3 0.7 %copy-start.2 = (f32[256]{0:T(256)S(1)}, f32[256]{0:T(256)}, u32[]{:S(2)}) copy-start(f32[256]{0:T(256)} %param.7) | copy-start | bytes 3076

commit v2 on v1

--- a/solution.py
+++ b/solution.py
@@ -11,6 +11,7 @@
 ITERS = 2
 CHUNKS = 4
 DENSE_LIMIT = 16 * 1024 * 1024
+VMEM_LIMIT = 64 * 1024 * 1024
 MESH = pl.DeviceIdType.MESH
 
 
@@ -94,15 +95,39 @@
 
 
 def densify_kernel(
-    rows_ref, cols_ref, count_ref, tiles_hbm, w_ref, row_ref, col_ref, tiles, dense, sems
+    rows_hbm,
+    cols_hbm,
+    count_hbm,
+    tiles_hbm,
+    w_hbm,
+    row_hbm,
+    col_hbm,
+    w_ref,
+    row_ref,
+    col_ref,
+    rows_ref,
+    cols_ref,
+    count_ref,
+    tiles,
+    dense,
+    small_sems,
+    sems,
+    out_sems,
 ):
     slots, side, _ = tiles.shape
     row_blocks = w_ref.shape[0] // side
     col_blocks = w_ref.shape[1] // side
     chunk = slots // CHUNKS
+    small = [
+        pltpu.make_async_copy(rows_hbm, rows_ref, small_sems.at[0]),
+        pltpu.make_async_copy(cols_hbm, cols_ref, small_sems.at[1]),
+        pltpu.make_async_copy(count_hbm, count_ref, small_sems.at[2]),
+    ]
+    for copy in small:
+        copy.start()
     copies = [
         pltpu.make_async_copy(
-            tiles_hbm.at[pl.ds(k * chunk, chunk)], tiles.at[pl.ds(k * chunk, chunk)], sems.at[k]
+            tiles_hbm.at[0, 0, pl.ds(k * chunk, chunk)], tiles.at[pl.ds(k * chunk, chunk)], sems.at[k]
         )
         for k in range(CHUNKS)
     ]
@@ -114,10 +139,12 @@
         return carry
 
     lax.fori_loop(0, row_blocks * col_blocks, clear, 0)
-    count = count_ref[0]
+    for copy in small:
+        copy.wait()
+    count = count_ref[0, 0]
 
     def add(s, carry):
-        place = rows_ref[s] * col_blocks + cols_ref[s]
+        place = rows_ref[0, 0, s] * col_blocks + cols_ref[0, 0, s]
         dense[place] += tiles[s].astype(jnp.float32)
         return carry
 
@@ -125,6 +152,7 @@
         copies[k].wait()
         lax.fori_loop(k * chunk, jnp.clip(count, k * chunk, (k + 1) * chunk), add, 0)
 
+    results = []
     col_sums = [jnp.zeros((8, side), jnp.float32) for _ in range(col_blocks)]
     for r in range(row_blocks):
         row_sum = jnp.zeros((side, side), jnp.float32)
@@ -135,9 +163,18 @@
             col_sums[c] = col_sums[c] + jnp.sum(block.reshape(side // 8, 8, side), axis=0)
         at = (r % NB_DEV) * side
         row_ref[r // NB_DEV, :, at : at + side] = jnp.sum(row_sum.T, axis=0, keepdims=True)
+        strip = pl.ds(r * side, side)
+        results.append(pltpu.make_async_copy(w_ref.at[strip], w_hbm.at[strip], out_sems.at[r]))
+        results[-1].start()
     for c in range(col_blocks):
         at = (c % NB_DEV) * side
         col_ref[c // NB_DEV, :, at : at + side] = jnp.sum(col_sums[c], axis=0, keepdims=True)
+    results.append(pltpu.make_async_copy(row_ref, row_hbm, small_sems.at[0]))
+    results.append(pltpu.make_async_copy(col_ref, col_hbm, small_sems.at[1]))
+    for copy in results[-2:]:
+        copy.start()
+    for copy in results:
+        copy.wait()
 
 
 def split(panel):
@@ -149,14 +186,18 @@
 def solve_kernel(
     n_clu,
     n_mem,
+    class_hbm,
+    weight_hbm,
+    w_hbm,
+    row_hbm,
+    col_hbm,
+    scores_ref,
+    residual_ref,
     class_ref,
     weight_ref,
-    w_hbm,
+    w,
     row_ref,
     col_ref,
-    scores_ref,
-    residual_ref,
-    w,
     deg_m,
     deg_c,
     own,
@@ -167,47 +208,47 @@
     got_m,
     got_c,
     dots,
-    got_dots,
-    w_sem,
+    dots_m,
+    dots_c,
+    load_sems,
     send_m,
     recv_m,
     send_c,
     recv_c,
-    send_d,
-    recv_d,
 ):
     me_c = lax.axis_index("clu")
     me_m = lax.axis_index("mem")
-    total = n_clu * n_mem
-    place = me_c * n_mem + me_m
-
-    def member(k):
-        other = lax.rem(place + k, total)
-        return (lax.div(other, n_mem), lax.rem(other, n_mem))
-
-    w_copy = pltpu.make_async_copy(w_hbm, w, w_sem)
+    others_m = [None] + [lax.rem(me_m + k, n_mem) for k in range(1, n_mem)]
+    others_c = [None] + [lax.rem(me_c + k, n_clu) for k in range(1, n_clu)]
+
+    loads = [
+        pltpu.make_async_copy(class_hbm, class_ref, load_sems.at[0]),
+        pltpu.make_async_copy(weight_hbm, weight_ref, load_sems.at[1]),
+        pltpu.make_async_copy(row_hbm, row_ref, load_sems.at[2]),
+        pltpu.make_async_copy(col_hbm, col_ref, load_sems.at[3]),
+    ]
+    w_copy = pltpu.make_async_copy(w_hbm, w, load_sems.at[4])
+    for copy in loads:
+        copy.start()
     w_copy.start()
     barrier = pltpu.get_barrier_semaphore()
-
-    def greet(k, carry):
-        pl.semaphore_signal(barrier, inc=1, device_id=member(k), device_id_type=MESH)
-        return carry
-
-    lax.fori_loop(1, total, greet, 0)
+    for k in range(1, n_mem):
+        pl.semaphore_signal(barrier, device_id=(me_c, others_m[k]), device_id_type=MESH)
+    for k in range(1, n_clu):
+        pl.semaphore_signal(barrier, device_id=(others_c[k], me_m), device_id_type=MESH)
 
     sent = []
 
     def over_mem(phase, source, target):
         copies = []
         for k in range(1, n_mem):
-            other = lax.rem(me_m + k, n_mem)
             copies.append(
                 pltpu.make_async_remote_copy(
-                    src_ref=source(other),
+                    src_ref=source(others_m[k]),
                     dst_ref=target(k),
                     send_sem=send_m.at[phase, k],
                     recv_sem=recv_m.at[phase, k],
-                    device_id=(me_c, other),
+                    device_id=(me_c, others_m[k]),
                     device_id_type=MESH,
                 )
             )
@@ -218,14 +259,13 @@
     def over_clu(phase, source, target):
         copies = []
         for k in range(1, n_clu):
-            other = lax.rem(me_c + k, n_clu)
             copies.append(
                 pltpu.make_async_remote_copy(
-                    src_ref=source(other),
+                    src_ref=source(others_c[k]),
                     dst_ref=target(k),
                     send_sem=send_c.at[phase, k],
                     recv_sem=recv_c.at[phase, k],
-                    device_id=(other, me_m),
+                    device_id=(others_c[k], me_m),
                     device_id_type=MESH,
                 )
             )
@@ -237,10 +277,12 @@
         for copy in copies:
             copy.wait_recv()
 
+    for copy in loads:
+        copy.wait()
     weight = weight_ref[...]
     kinds = lax.broadcasted_iota(jnp.int32, (CLASSES, weight.shape[1]), 0)
     labels = jnp.where(class_ref[...] == kinds, weight, jnp.float32(0.0))
-    pl.semaphore_wait(barrier, total - 1)
+    pl.semaphore_wait(barrier, n_mem + n_clu - 2)
 
     from_m = over_mem(0, lambda o: row_ref.at[o], lambda k: deg_m.at[k])
     from_c = over_clu(0, lambda o: col_ref.at[o], lambda k: deg_c.at[k])
@@ -261,7 +303,7 @@
         from_c = over_clu(1 + 2 * step, lambda o: own.at[step], lambda k: pan_c.at[step, me_c])
         return from_m, from_c
 
-    def multiply(step, from_m, from_c, prepare):
+    def multiply(step, from_m, from_c, prepare, between):
         phase = 2 + 2 * step
         arrive(from_m)
         left = jnp.concatenate([pan_m[step, k] for k in range(n_mem)], axis=1)
@@ -277,6 +319,7 @@
         back_c = over_clu(phase, lambda o: part_c.at[step, o], lambda k: got_c.at[step, k])
         arrive(from_c)
         right = jnp.concatenate([pan_c[step, k] for k in range(n_clu)], axis=1)
+        between(right, out)
         out = lax.dot_general(
             prepare(right), w[...], (((1,), (1,)), ((), ())), preferred_element_type=jnp.float32
         )
@@ -284,7 +327,7 @@
         for k in range(n_mem):
             part_m[step, k] = out[:, k * width : (k + 1) * width]
         back_m = over_mem(phase, lambda o: part_m.at[step, o], lambda k: got_m.at[step, k])
-        return back_m, back_c, jnp.sum(left * out, axis=1, keepdims=True)
+        return back_m, back_c
 
     def collect(step, back_m, back_c):
         image = part_m[step, me_m] + part_c[step, me_c]
@@ -297,47 +340,40 @@
         return 0.99 * root * image
 
     from_m, from_c = gather(0, root * labels)
-    back_m, back_c, _ = multiply(0, from_m, from_c, lambda x: x.astype(jnp.bfloat16))
+    back_m, back_c = multiply(
+        0, from_m, from_c, lambda x: x.astype(jnp.bfloat16), lambda right, out: None
+    )
     first = collect(0, back_m, back_c)
 
     from_m, from_c = gather(1, root * first)
+    lane = lax.broadcasted_iota(jnp.int32, (CLASSES, 128), 1)
+    kind = lax.broadcasted_iota(jnp.int32, (CLASSES, 128), 0)
     sums = [
         jnp.sum(labels * labels, axis=1, keepdims=True),
         jnp.sum(labels * first, axis=1, keepdims=True),
         jnp.sum(first * first, axis=1, keepdims=True),
     ]
-    back_m, back_c, cross = multiply(1, from_m, from_c, split)
-    sums.append(1.98 * cross)
-
-    lane = lax.broadcasted_iota(jnp.int32, (CLASSES, 128), 1)
-    kind = lax.broadcasted_iota(jnp.int32, (CLASSES, 128), 0)
-    line = jnp.zeros((CLASSES, 128), jnp.float32)
-    for k, value in enumerate(sums):
-        line = line + jnp.where(lane == kind + k * CLASSES, value, 0.0)
-    line = jnp.sum(line, axis=0, keepdims=True)
-    dots[...] = line
-
-    def dot_copy(k):
-        return pltpu.make_async_remote_copy(
-            src_ref=dots,
-            dst_ref=got_dots.at[k],
-            send_sem=send_d.at[k],
-            recv_sem=recv_d.at[k],
-            device_id=member(k),
-            device_id_type=MESH,
-        )
-
-    def send_dot(k, carry):
-        dot_copy(k).start()
-        return carry
-
-    def take_dot(k, carry):
-        dot_copy(k).wait_recv()
-        return carry + got_dots[k]
-
-    lax.fori_loop(1, total, send_dot, 0)
+    dot_copies = []
+
+    def send_sums(right, image):
+        cross = 1.98 * jnp.sum(right * image, axis=1, keepdims=True)
+        line = jnp.zeros((CLASSES, 128), jnp.float32)
+        for k, value in enumerate([*sums, cross]):
+            line = line + jnp.where(lane == kind + k * CLASSES, value, 0.0)
+        dots[0] = jnp.sum(line, axis=0, keepdims=True)
+        dot_copies.extend(over_mem(5, lambda o: dots.at[0], lambda k: dots_m.at[k]))
+
+    back_m, back_c = multiply(1, from_m, from_c, split, send_sums)
+    arrive(dot_copies)
+    line = dots[0]
+    for k in range(1, n_mem):
+        line = line + dots_m[k]
+    dots[1] = line
+    dot_copies = over_clu(5, lambda o: dots.at[1], lambda k: dots_c.at[k])
     second = collect(1, back_m, back_c)
-    line = lax.fori_loop(1, total, take_dot, line)
+    arrive(dot_copies)
+    for k in range(1, n_clu):
+        line = line + dots_c[k]
     spread_line = jnp.broadcast_to(line, (CLASSES, 128))
     bb, bq, qq, qt = [
         jnp.sum(
@@ -357,11 +393,6 @@
     scores_ref[...] = alpha * labels + alpha_next * direction
     residual_ref[...] = alpha * (first - ratio * labels) - alpha_next * image
 
-    def leave_dot(k, carry):
-        dot_copy(k).wait_send()
-        return carry
-
-    lax.fori_loop(1, total, leave_dot, 0)
     for copy in sent:
         copy.wait_send()
 
@@ -369,15 +400,13 @@
 def on_device_dense(seed_class, seed_weight, tile_values, tile_rows, tile_cols, tile_count):
     n_clu = lax.axis_size("clu")
     n_mem = lax.axis_size("mem")
-    tiles = tile_values[0, 0]
-    slots, side, _ = tiles.shape
+    _, _, slots, side, _ = tile_values.shape
     nodes = NB_DEV * side
     rows = nodes * n_mem
     cols = nodes * n_clu
     f32 = jnp.float32
-    smem = pl.BlockSpec(memory_space=pltpu.SMEM)
     vmem = pl.BlockSpec(memory_space=pltpu.VMEM)
-    hbm = pl.BlockSpec(memory_space=pl.ANY)
+    hbm = pl.BlockSpec(memory_space=pltpu.HBM)
     w, row_total, col_total = pl.pallas_call(
         densify_kernel,
         out_shape=(
@@ -385,25 +414,37 @@
             jax.ShapeDtypeStruct((n_mem, 1, nodes), f32),
             jax.ShapeDtypeStruct((n_clu, 1, nodes), f32),
         ),
-        in_specs=[smem, smem, smem, hbm],
-        out_specs=(vmem, vmem, vmem),
+        in_specs=[hbm, hbm, hbm, hbm],
+        out_specs=(hbm, hbm, hbm),
         scratch_shapes=[
-            pltpu.VMEM((slots, side, side), tiles.dtype),
+            pltpu.VMEM((rows, cols), jnp.bfloat16),
+            pltpu.VMEM((n_mem, 1, nodes), f32),
+            pltpu.VMEM((n_clu, 1, nodes), f32),
+            pltpu.SMEM(tile_rows.shape, jnp.int32),
+            pltpu.SMEM(tile_cols.shape, jnp.int32),
+            pltpu.SMEM(tile_count.shape, jnp.int32),
+            pltpu.VMEM((slots, side, side), tile_values.dtype),
             pltpu.VMEM((rows * cols // (side * side), side, side), f32),
+            pltpu.SemaphoreType.DMA((3,)),
             pltpu.SemaphoreType.DMA((CHUNKS,)),
+            pltpu.SemaphoreType.DMA((rows // side,)),
         ],
-        compiler_params=pltpu.CompilerParams(vmem_limit_bytes=24 * 1024 * 1024),
+        compiler_params=pltpu.CompilerParams(vmem_limit_bytes=VMEM_LIMIT),
         name="densify",
-    )(tile_rows[0, 0], tile_cols[0, 0], tile_count[0], tiles)
+    )(tile_rows, tile_cols, tile_count, tile_values)
     panel = (CLASSES, nodes)
     dma = pltpu.SemaphoreType.DMA
     return pl.pallas_call(
         functools.partial(solve_kernel, n_clu, n_mem),
         out_shape=(jax.ShapeDtypeStruct(panel, f32), jax.ShapeDtypeStruct(panel, f32)),
-        in_specs=[vmem, vmem, hbm, vmem, vmem],
+        in_specs=[hbm, hbm, hbm, hbm, hbm],
         out_specs=(vmem, vmem),
         scratch_shapes=[
+            pltpu.VMEM((1, nodes), jnp.int32),
+            pltpu.VMEM((1, nodes), f32),
             pltpu.VMEM((rows, cols), jnp.bfloat16),
+            pltpu.VMEM((n_mem, 1, nodes), f32),
+            pltpu.VMEM((n_clu, 1, nodes), f32),
             pltpu.VMEM((n_mem, 1, nodes), f32),
             pltpu.VMEM((n_clu, 1, nodes), f32),
             pltpu.VMEM((ITERS, *panel), f32),
@@ -413,18 +454,17 @@
             pltpu.VMEM((ITERS, n_clu, *panel), f32),
             pltpu.VMEM((ITERS, n_mem, *panel), f32),
             pltpu.VMEM((ITERS, n_clu, *panel), f32),
-            pltpu.VMEM((1, 128), f32),
-            pltpu.VMEM((n_clu * n_mem, 1, 128), f32),
-            dma,
-            dma((1 + 2 * ITERS, n_mem)),
-            dma((1 + 2 * ITERS, n_mem)),
-            dma((1 + 2 * ITERS, n_clu)),
-            dma((1 + 2 * ITERS, n_clu)),
-            dma((n_clu * n_mem,)),
-            dma((n_clu * n_mem,)),
+            pltpu.VMEM((2, 1, 128), f32),
+            pltpu.VMEM((n_mem, 1, 128), f32),
+            pltpu.VMEM((n_clu, 1, 128), f32),
+            dma((5,)),
+            dma((2 + 2 * ITERS, n_mem)),
+            dma((2 + 2 * ITERS, n_mem)),
+            dma((2 + 2 * ITERS, n_clu)),
+            dma((2 + 2 * ITERS, n_clu)),
         ],
         compiler_params=pltpu.CompilerParams(
-            collective_id=0, has_side_effects=True, vmem_limit_bytes=16 * 1024 * 1024
+            collective_id=0, has_side_effects=True, vmem_limit_bytes=VMEM_LIMIT
         ),
         name="solve",
     )(seed_class[None], seed_weight[None], w, row_total, col_total)

time: 42.6 us -> 40.1 us (0.941)
  local copies, waits for them, and re-layouts: 5.74 us -> 2.59 us
  Pallas kernels: 35.2 us -> 36 us
    unnamed x12 -> x2, local copies, waits for them, and re-layouts: 5.74 us -> 2.59 us
    pallas_call x1, Pallas kernels: 3.15 us -> 5.34 us  [on_device_dense(): pl.pallas_call(densify_kernel, out_shape=(jax.ShapeDtypeStruct((rows, col...]
    pallas_call x1, Pallas kernels: 32 us -> 30.7 us  [on_device_dense(): pl.pallas_call(functools.partial(solve_kernel, n_clu, n_mem), out_shape=(...]
where the time goes in v2:
time: 40.1 us; the launch traced here: 39.9 us
  Pallas kernels  36 us (90%)
  local copies, waits for them, and re-layouts  2.59 us (6%)
  between operations  1.29 us (3%)
    pallas_call x1, Pallas kernels, on_device_dense(): pl.pallas_call(functools.partial(solve_kernel, n_clu, n_mem), out_shape=(...  30.7 us
    pallas_call x1, Pallas kernels, on_device_dense(): pl.pallas_call(densify_kernel, out_shape=(jax.ShapeDtypeStruct((rows, col...  5.34 us
    unnamed x2, local copies, waits for them, and re-layouts  2.59 us

profile of v2, /device:TPU:0, one launch (start us, length us, event | category | flops | bytes accessed | tf_op | source)
XLA Modules:
  0.0 39.9 jit_solution(132827799097515737)
XLA Ops:
  1.3 5.3 %densify.1 = (bf16[1024,2048]{1,0:T(8,128)(2,1)}, f32[4,1,256]{2,1,0:T(1,128)}, f32[8,1,256]{2,1,0:T(1,128)}) custom-call(s32[1,1,96]{2,1,0:T(1,128)} %rows_hbm.1, s32[1,1,96]{2,1,0:T(1,128)} %cols_hbm.1, s32[1,1]{1,0:T(1,128)S(6)} %copy.10.count_hbm, bf16[1,1,96,128,128]{4,3,2,1,0:T(8,128)(2,1)} %tiles_hbm.1), custom_call_target="tpu_custom_call" | custom-call | tf_op jit(solution)/shard_map/densify/pallas_call | solution.py:410
  6.6 30.7 %solve.1 = (f32[8,256]{1,0:T(8,128)}, f32[8,256]{1,0:T(8,128)}) custom-call(s32[1,256]{1,0:T(1,128)} %bitcast.2, f32[1,256]{1,0:T(1,128)} %bitcast.3, bf16[1024,2048]{1,0:T(8,128)(2,1)} %get-tuple-element.5.w_hbm, f32[4,1,256]{2,1,0:T(1,128)} %get-tuple-element.6.row_hbm, f32[8,1,256]{2,1,0:T(1,128)} %get-tuple-element.7.col_hbm), custom_call_target="tpu_custom_call" | custom-call | tf_op jit(solution)/shard_map/solve/pallas_call | solution.py:437
  37.3 1.3 %copy.11 = f32[8,256]{1,0:T(8,128)} copy(f32[8,256]{1,0:T(8,128)} %get-tuple-element.10) | data formatting | bytes 16384
  38.6 1.3 %copy.12 = f32[8,256]{1,0:T(8,128)} copy(f32[8,256]{1,0:T(8,128)} %get-tuple-element.11) | data formatting | bytes 16384

commit v3 on v2

--- a/solution.py
+++ b/solution.py
@@ -99,12 +99,16 @@
     cols_hbm,
     count_hbm,
     tiles_hbm,
+    class_hbm,
+    weight_hbm,
     w_hbm,
-    row_hbm,
-    col_hbm,
+    sums_hbm,
+    labels_hbm,
     w_ref,
-    row_ref,
-    col_ref,
+    sums_ref,
+    labels_ref,
+    class_ref,
+    weight_ref,
     rows_ref,
     cols_ref,
     count_ref,
@@ -122,6 +126,8 @@
         pltpu.make_async_copy(rows_hbm, rows_ref, small_sems.at[0]),
         pltpu.make_async_copy(cols_hbm, cols_ref, small_sems.at[1]),
         pltpu.make_async_copy(count_hbm, count_ref, small_sems.at[2]),
+        pltpu.make_async_copy(class_hbm, class_ref, small_sems.at[3]),
+        pltpu.make_async_copy(weight_hbm, weight_ref, small_sems.at[4]),
     ]
     for copy in small:
         copy.start()
@@ -142,6 +148,12 @@
     for copy in small:
         copy.wait()
     count = count_ref[0, 0]
+    kinds = lax.broadcasted_iota(jnp.int32, labels_ref.shape, 0)
+    labels_ref[...] = jnp.where(class_ref[...] == kinds, weight_ref[...], jnp.float32(0.0))
+    results = [
+        pltpu.make_async_copy(labels_ref, labels_hbm, small_sems.at[0])
+    ]
+    results[0].start()
 
     def add(s, carry):
         place = rows_ref[0, 0, s] * col_blocks + cols_ref[0, 0, s]
@@ -152,7 +164,7 @@
         copies[k].wait()
         lax.fori_loop(k * chunk, jnp.clip(count, k * chunk, (k + 1) * chunk), add, 0)
 
-    results = []
+    members = row_blocks // NB_DEV
     col_sums = [jnp.zeros((8, side), jnp.float32) for _ in range(col_blocks)]
     for r in range(row_blocks):
         row_sum = jnp.zeros((side, side), jnp.float32)
@@ -162,17 +174,15 @@
             row_sum = row_sum + block
             col_sums[c] = col_sums[c] + jnp.sum(block.reshape(side // 8, 8, side), axis=0)
         at = (r % NB_DEV) * side
-        row_ref[r // NB_DEV, :, at : at + side] = jnp.sum(row_sum.T, axis=0, keepdims=True)
+        sums_ref[r // NB_DEV, :, at : at + side] = jnp.sum(row_sum.T, axis=0, keepdims=True)
         strip = pl.ds(r * side, side)
         results.append(pltpu.make_async_copy(w_ref.at[strip], w_hbm.at[strip], out_sems.at[r]))
         results[-1].start()
     for c in range(col_blocks):
         at = (c % NB_DEV) * side
-        col_ref[c // NB_DEV, :, at : at + side] = jnp.sum(col_sums[c], axis=0, keepdims=True)
-    results.append(pltpu.make_async_copy(row_ref, row_hbm, small_sems.at[0]))
-    results.append(pltpu.make_async_copy(col_ref, col_hbm, small_sems.at[1]))
-    for copy in results[-2:]:
-        copy.start()
+        sums_ref[members + c // NB_DEV, :, at : at + side] = jnp.sum(col_sums[c], axis=0, keepdims=True)
+    results.append(pltpu.make_async_copy(sums_ref, sums_hbm, small_sems.at[1]))
+    results[-1].start()
     for copy in results:
         copy.wait()
 
@@ -186,18 +196,14 @@
 def solve_kernel(
     n_clu,
     n_mem,
-    class_hbm,
-    weight_hbm,
     w_hbm,
-    row_hbm,
-    col_hbm,
+    sums_hbm,
+    labels_hbm,
     scores_ref,
     residual_ref,
-    class_ref,
-    weight_ref,
     w,
-    row_ref,
-    col_ref,
+    sums_ref,
+    labels_ref,
     deg_m,
     deg_c,
     own,
@@ -222,12 +228,10 @@
     others_c = [None] + [lax.rem(me_c + k, n_clu) for k in range(1, n_clu)]
 
     loads = [
-        pltpu.make_async_copy(class_hbm, class_ref, load_sems.at[0]),
-        pltpu.make_async_copy(weight_hbm, weight_ref, load_sems.at[1]),
-        pltpu.make_async_copy(row_hbm, row_ref, load_sems.at[2]),
-        pltpu.make_async_copy(col_hbm, col_ref, load_sems.at[3]),
-    ]
-    w_copy = pltpu.make_async_copy(w_hbm, w, load_sems.at[4])
+        pltpu.make_async_copy(sums_hbm, sums_ref, load_sems.at[0]),
+        pltpu.make_async_copy(labels_hbm, labels_ref, load_sems.at[1]),
+    ]
+    w_copy = pltpu.make_async_copy(w_hbm, w, load_sems.at[2])
     for copy in loads:
         copy.start()
     w_copy.start()
@@ -239,58 +243,47 @@
 
     sent = []
 
-    def over_mem(phase, source, target):
-        copies = []
+    def whole(room, count, send_sem, recv_sem):
+        view = room.at[pl.ds(0, count - 1)]
+        sent.append(pltpu.make_async_copy(view, view, send_sem))
+        return pltpu.make_async_copy(view, view, recv_sem)
+
+    def over_mem(phase, source, target, room):
         for k in range(1, n_mem):
-            copies.append(
-                pltpu.make_async_remote_copy(
-                    src_ref=source(others_m[k]),
-                    dst_ref=target(k),
-                    send_sem=send_m.at[phase, k],
-                    recv_sem=recv_m.at[phase, k],
-                    device_id=(me_c, others_m[k]),
-                    device_id_type=MESH,
-                )
-            )
-            copies[-1].start()
-        sent.extend(copies)
-        return copies
-
-    def over_clu(phase, source, target):
-        copies = []
+            pltpu.make_async_remote_copy(
+                src_ref=source(others_m[k]),
+                dst_ref=target(k),
+                send_sem=send_m.at[phase],
+                recv_sem=recv_m.at[phase],
+                device_id=(me_c, others_m[k]),
+                device_id_type=MESH,
+            ).start()
+        return whole(room, n_mem, send_m.at[phase], recv_m.at[phase])
+
+    def over_clu(phase, source, target, room):
         for k in range(1, n_clu):
-            copies.append(
-                pltpu.make_async_remote_copy(
-                    src_ref=source(others_c[k]),
-                    dst_ref=target(k),
-                    send_sem=send_c.at[phase, k],
-                    recv_sem=recv_c.at[phase, k],
-                    device_id=(others_c[k], me_m),
-                    device_id_type=MESH,
-                )
-            )
-            copies[-1].start()
-        sent.extend(copies)
-        return copies
-
-    def arrive(copies):
-        for copy in copies:
-            copy.wait_recv()
+            pltpu.make_async_remote_copy(
+                src_ref=source(others_c[k]),
+                dst_ref=target(k),
+                send_sem=send_c.at[phase],
+                recv_sem=recv_c.at[phase],
+                device_id=(others_c[k], me_m),
+                device_id_type=MESH,
+            ).start()
+        return whole(room, n_clu, send_c.at[phase], recv_c.at[phase])
 
     for copy in loads:
         copy.wait()
-    weight = weight_ref[...]
-    kinds = lax.broadcasted_iota(jnp.int32, (CLASSES, weight.shape[1]), 0)
-    labels = jnp.where(class_ref[...] == kinds, weight, jnp.float32(0.0))
+    labels = labels_ref[...]
     pl.semaphore_wait(barrier, n_mem + n_clu - 2)
 
-    from_m = over_mem(0, lambda o: row_ref.at[o], lambda k: deg_m.at[k])
-    from_c = over_clu(0, lambda o: col_ref.at[o], lambda k: deg_c.at[k])
-    degree = 1.0 + (row_ref[me_m] + col_ref[me_c])
-    arrive(from_m)
+    from_m = over_mem(0, lambda o: sums_ref.at[o], lambda k: deg_m.at[k], deg_m)
+    from_c = over_clu(0, lambda o: sums_ref.at[n_mem + o], lambda k: deg_c.at[k], deg_c)
+    degree = 1.0 + (sums_ref[me_m] + sums_ref[n_mem + me_c])
+    from_m.wait()
     for k in range(1, n_mem):
         degree = degree + deg_m[k]
-    arrive(from_c)
+    from_c.wait()
     for k in range(1, n_clu):
         degree = degree + deg_c[k]
     root = lax.rsqrt(degree)
@@ -299,13 +292,13 @@
         own[step] = panel
         pan_m[step, me_m] = panel
         pan_c[step, me_c] = panel
-        from_m = over_mem(1 + 2 * step, lambda o: own.at[step], lambda k: pan_m.at[step, me_m])
-        from_c = over_clu(1 + 2 * step, lambda o: own.at[step], lambda k: pan_c.at[step, me_c])
+        from_m = over_mem(1 + 2 * step, lambda o: own.at[step], lambda k: pan_m.at[step, me_m], pan_m.at[step])
+        from_c = over_clu(1 + 2 * step, lambda o: own.at[step], lambda k: pan_c.at[step, me_c], pan_c.at[step])
         return from_m, from_c
 
     def multiply(step, from_m, from_c, prepare, between):
         phase = 2 + 2 * step
-        arrive(from_m)
+        from_m.wait()
         left = jnp.concatenate([pan_m[step, k] for k in range(n_mem)], axis=1)
         if step == 0:
             w_copy.wait()
@@ -316,8 +309,8 @@
         width = out.shape[1] // n_clu
         for k in range(n_clu):
             part_c[step, k] = out[:, k * width : (k + 1) * width]
-        back_c = over_clu(phase, lambda o: part_c.at[step, o], lambda k: got_c.at[step, k])
-        arrive(from_c)
+        back_c = over_clu(phase, lambda o: part_c.at[step, o], lambda k: got_c.at[step, k], got_c.at[step])
+        from_c.wait()
         right = jnp.concatenate([pan_c[step, k] for k in range(n_clu)], axis=1)
         between(right, out)
         out = lax.dot_general(
@@ -326,15 +319,15 @@
         out = out[:CLASSES] if step == 0 else out[:CLASSES] + out[CLASSES:]
         for k in range(n_mem):
             part_m[step, k] = out[:, k * width : (k + 1) * width]
-        back_m = over_mem(phase, lambda o: part_m.at[step, o], lambda k: got_m.at[step, k])
+        back_m = over_mem(phase, lambda o: part_m.at[step, o], lambda k: got_m.at[step, k], got_m.at[step])
         return back_m, back_c
 
     def collect(step, back_m, back_c):
         image = part_m[step, me_m] + part_c[step, me_c]
-        arrive(back_c)
+        back_c.wait()
         for k in range(1, n_clu):
             image = image + got_c[step, k]
-        arrive(back_m)
+        back_m.wait()
         for k in range(1, n_mem):
             image = image + got_m[step, k]
         return 0.99 * root * image
@@ -361,17 +354,17 @@
         for k, value in enumerate([*sums, cross]):
             line = line + jnp.where(lane == kind + k * CLASSES, value, 0.0)
         dots[0] = jnp.sum(line, axis=0, keepdims=True)
-        dot_copies.extend(over_mem(5, lambda o: dots.at[0], lambda k: dots_m.at[k]))
+        dot_copies.append(over_mem(5, lambda o: dots.at[0], lambda k: dots_m.at[k], dots_m))
 
     back_m, back_c = multiply(1, from_m, from_c, split, send_sums)
-    arrive(dot_copies)
+    dot_copies[0].wait()
     line = dots[0]
     for k in range(1, n_mem):
         line = line + dots_m[k]
     dots[1] = line
-    dot_copies = over_clu(5, lambda o: dots.at[1], lambda k: dots_c.at[k])
+    dot_copies.append(over_clu(5, lambda o: dots.at[1], lambda k: dots_c.at[k], dots_c))
     second = collect(1, back_m, back_c)
-    arrive(dot_copies)
+    dot_copies[1].wait()
     for k in range(1, n_clu):
         line = line + dots_c[k]
     spread_line = jnp.broadcast_to(line, (CLASSES, 128))
@@ -394,7 +387,18 @@
     residual_ref[...] = alpha * (first - ratio * labels) - alpha_next * image
 
     for copy in sent:
-        copy.wait_send()
+        copy.wait()
+
+
+def finish_kernel(scores_in, residual_in, scores_out, residual_out, sems):
+    copies = [
+        pltpu.make_async_copy(scores_in, scores_out, sems.at[0]),
+        pltpu.make_async_copy(residual_in, residual_out, sems.at[1]),
+    ]
+    for copy in copies:
+        copy.start()
+    for copy in copies:
+        copy.wait()
 
 
 def on_device_dense(seed_class, seed_weight, tile_values, tile_rows, tile_cols, tile_count):
@@ -407,44 +411,45 @@
     f32 = jnp.float32
     vmem = pl.BlockSpec(memory_space=pltpu.VMEM)
     hbm = pl.BlockSpec(memory_space=pltpu.HBM)
-    w, row_total, col_total = pl.pallas_call(
+    panel = (CLASSES, nodes)
+    w, sums, labels = pl.pallas_call(
         densify_kernel,
         out_shape=(
             jax.ShapeDtypeStruct((rows, cols), jnp.bfloat16),
-            jax.ShapeDtypeStruct((n_mem, 1, nodes), f32),
-            jax.ShapeDtypeStruct((n_clu, 1, nodes), f32),
+            jax.ShapeDtypeStruct((n_mem + n_clu, 1, nodes), f32),
+            jax.ShapeDtypeStruct(panel, f32),
         ),
-        in_specs=[hbm, hbm, hbm, hbm],
+        in_specs=[hbm] * 6,
         out_specs=(hbm, hbm, hbm),
         scratch_shapes=[
             pltpu.VMEM((rows, cols), jnp.bfloat16),
-            pltpu.VMEM((n_mem, 1, nodes), f32),
-            pltpu.VMEM((n_clu, 1, nodes), f32),
+            pltpu.VMEM((n_mem + n_clu, 1, nodes), f32),
+            pltpu.VMEM(panel, f32),
+            pltpu.VMEM((1, nodes), jnp.int32),
+            pltpu.VMEM((1, nodes), f32),
             pltpu.SMEM(tile_rows.shape, jnp.int32),
             pltpu.SMEM(tile_cols.shape, jnp.int32),
             pltpu.SMEM(tile_count.shape, jnp.int32),
             pltpu.VMEM((slots, side, side), tile_values.dtype),
             pltpu.VMEM((rows * cols // (side * side), side, side), f32),
-            pltpu.SemaphoreType.DMA((3,)),
+            pltpu.SemaphoreType.DMA((5,)),
             pltpu.SemaphoreType.DMA((CHUNKS,)),
             pltpu.SemaphoreType.DMA((rows // side,)),
         ],
         compiler_params=pltpu.CompilerParams(vmem_limit_bytes=VMEM_LIMIT),
         name="densify",
-    )(tile_rows, tile_cols, tile_count, tile_values)
-    panel = (CLASSES, nodes)
+    )(tile_rows, tile_cols, tile_count, tile_values, seed_class[None], seed_weight[None])
     dma = pltpu.SemaphoreType.DMA
-    return pl.pallas_call(
+    results = (jax.ShapeDtypeStruct(panel, f32), jax.ShapeDtypeStruct(panel, f32))
+    found = pl.pallas_call(
         functools.partial(solve_kernel, n_clu, n_mem),
-        out_shape=(jax.ShapeDtypeStruct(panel, f32), jax.ShapeDtypeStruct(panel, f32)),
-        in_specs=[hbm, hbm, hbm, hbm, hbm],
+        out_shape=results,
+        in_specs=[hbm] * 3,
         out_specs=(vmem, vmem),
         scratch_shapes=[
-            pltpu.VMEM((1, nodes), jnp.int32),
-            pltpu.VMEM((1, nodes), f32),
             pltpu.VMEM((rows, cols), jnp.bfloat16),
-            pltpu.VMEM((n_mem, 1, nodes), f32),
-            pltpu.VMEM((n_clu, 1, nodes), f32),
+            pltpu.VMEM((n_mem + n_clu, 1, nodes), f32),
+            pltpu.VMEM(panel, f32),
             pltpu.VMEM((n_mem, 1, nodes), f32),
             pltpu.VMEM((n_clu, 1, nodes), f32),
             pltpu.VMEM((ITERS, *panel), f32),
@@ -457,17 +462,26 @@
             pltpu.VMEM((2, 1, 128), f32),
             pltpu.VMEM((n_mem, 1, 128), f32),
             pltpu.VMEM((n_clu, 1, 128), f32),
-            dma((5,)),
-            dma((2 + 2 * ITERS, n_mem)),
-            dma((2 + 2 * ITERS, n_mem)),
-            dma((2 + 2 * ITERS, n_clu)),
-            dma((2 + 2 * ITERS, n_clu)),
+            dma((3,)),
+            dma((2 + 2 * ITERS,)),
+            dma((2 + 2 * ITERS,)),
+            dma((2 + 2 * ITERS,)),
+            dma((2 + 2 * ITERS,)),
         ],
         compiler_params=pltpu.CompilerParams(
             collective_id=0, has_side_effects=True, vmem_limit_bytes=VMEM_LIMIT
         ),
         name="solve",
-    )(seed_class[None], seed_weight[None], w, row_total, col_total)
+    )(w, sums, labels)
+    return pl.pallas_call(
+        finish_kernel,
+        out_shape=results,
+        in_specs=[hbm, hbm],
+        out_specs=(hbm, hbm),
+        scratch_shapes=[dma((2,))],
+        compiler_params=pltpu.CompilerParams(vmem_limit_bytes=VMEM_LIMIT),
+        name="finish",
+    )(*found)
 
 
 def on_device(seed_class, seed_weight, tile_values, tile_rows, tile_cols, tile_count):

time: 40.1 us -> 38.4 us (0.958)
  local copies, waits for them, and re-layouts: 2.59 us -> 0 us
  Pallas kernels: 36 us -> 36.8 us
    unnamed x2 -> x0, local copies, waits for them, and re-layouts: 2.59 us -> none
    pallas_call x1, Pallas kernels: 5.34 us -> 6.01 us  [on_device_dense(): pl.pallas_call(densify_kernel, out_shape=(jax.ShapeDtypeStruct((rows, col...]
    pallas_call x1 -> x2, Pallas kernels: 30.7 us -> 30.8 us  [the longest x1 29.2 us: on_device_dense(): pl.pallas_call(functools.partial(solve_kernel, n_clu, n_mem), out_shape=r...]
where the time goes in v3:
time: 38.4 us; the launch traced here: 38.1 us
  Pallas kernels  36.8 us (96%)
  between operations  1.29 us (3%)
    pallas_call x1, Pallas kernels, on_device_dense(): pl.pallas_call(functools.partial(solve_kernel, n_clu, n_mem), out_shape=r...  29.2 us
    pallas_call x1, Pallas kernels, on_device_dense(): pl.pallas_call(densify_kernel, out_shape=(jax.ShapeDtypeStruct((rows, col...  6.01 us
    pallas_call x1, Pallas kernels, on_device_dense(): pl.pallas_call(finish_kernel, out_shape=results, in_specs=[hbm, hbm], out...  1.62 us

profile of v3, /device:TPU:0, one launch (start us, length us, event | category | flops | bytes accessed | tf_op | source)
XLA Modules:
  0.0 38.1 jit_solution(3109507383852548846)
XLA Ops:
  1.3 6.0 %densify.1 = (bf16[1024,2048]{1,0:T(8,128)(2,1)}, f32[12,1,256]{2,1,0:T(1,128)}, f32[8,256]{1,0:T(8,128)}) custom-call(s32[1,1,96]{2,1,0:T(1,128)} %rows_hbm.1, s32[1,1,96]{2,1,0:T(1,128)} %cols_hbm.1, s32[1,1]{1,0:T(1,128)S(6)} %copy.8.count_hbm, bf16[1,1,96,128,128]{4,3,2,1,0:T(8,128)(2,1)} %tiles_hbm.1, s32[1,256]{1,0:T(1,128)} %bitcast.2, f32[1,256]{1,0:T(1,128)} %bitcast.3), custom_call_target="tpu_custom_call" | custom-call | tf_op jit(solution)/shard_map/densify/pallas_call | solution.py:415
  7.3 29.2 %solve.1 = (f32[8,256]{1,0:T(8,128)}, f32[8,256]{1,0:T(8,128)}) custom-call(bf16[1024,2048]{1,0:T(8,128)(2,1)} %get-tuple-element.7.w_hbm, f32[12,1,256]{2,1,0:T(1,128)} %get-tuple-element.8.sums_hbm, f32[8,256]{1,0:T(8,128)} %get-tuple-element.9.labels_hbm), custom_call_target="tpu_custom_call" | custom-call | tf_op jit(solution)/shard_map/solve/pallas_call | solution.py:444
  36.5 1.6 %finish.1 = (f32[8,256]{1,0:T(8,128)}, f32[8,256]{1,0:T(8,128)}) custom-call(f32[8,256]{1,0:T(8,128)} %get-tuple-element.10.scores_in, f32[8,256]{1,0:T(8,128)} %get-tuple-element.11.residual_in), custom_call_target="tpu_custom_call" | custom-call | tf_op jit(solution)/shard_map/finish/pallas_call | solution.py:476

commit v4 on v3

--- a/solution.py
+++ b/solution.py
@@ -9,8 +9,9 @@
 CLASSES = 8
 NB_DEV = 2
 ITERS = 2
-CHUNKS = 4
-DENSE_LIMIT = 16 * 1024 * 1024
+GROUP = 16
+PACK = 4
+TABLE_LIMIT = 16 * 1024 * 1024
 VMEM_LIMIT = 64 * 1024 * 1024
 MESH = pl.DeviceIdType.MESH
 
@@ -94,116 +95,28 @@
     return (scores, residual)
 
 
-def densify_kernel(
+def solve_kernel(
+    n_clu,
+    n_mem,
+    class_hbm,
+    weight_hbm,
+    tiles_hbm,
     rows_hbm,
     cols_hbm,
     count_hbm,
-    tiles_hbm,
-    class_hbm,
-    weight_hbm,
-    w_hbm,
-    sums_hbm,
-    labels_hbm,
-    w_ref,
-    sums_ref,
-    labels_ref,
+    scores_ref,
+    residual_ref,
     class_ref,
     weight_ref,
     rows_ref,
     cols_ref,
     count_ref,
     tiles,
-    dense,
-    small_sems,
-    sems,
-    out_sems,
-):
-    slots, side, _ = tiles.shape
-    row_blocks = w_ref.shape[0] // side
-    col_blocks = w_ref.shape[1] // side
-    chunk = slots // CHUNKS
-    small = [
-        pltpu.make_async_copy(rows_hbm, rows_ref, small_sems.at[0]),
-        pltpu.make_async_copy(cols_hbm, cols_ref, small_sems.at[1]),
-        pltpu.make_async_copy(count_hbm, count_ref, small_sems.at[2]),
-        pltpu.make_async_copy(class_hbm, class_ref, small_sems.at[3]),
-        pltpu.make_async_copy(weight_hbm, weight_ref, small_sems.at[4]),
-    ]
-    for copy in small:
-        copy.start()
-    copies = [
-        pltpu.make_async_copy(
-            tiles_hbm.at[0, 0, pl.ds(k * chunk, chunk)], tiles.at[pl.ds(k * chunk, chunk)], sems.at[k]
-        )
-        for k in range(CHUNKS)
-    ]
-    for copy in copies:
-        copy.start()
-
-    def clear(k, carry):
-        dense[k] = jnp.zeros((side, side), jnp.float32)
-        return carry
-
-    lax.fori_loop(0, row_blocks * col_blocks, clear, 0)
-    for copy in small:
-        copy.wait()
-    count = count_ref[0, 0]
-    kinds = lax.broadcasted_iota(jnp.int32, labels_ref.shape, 0)
-    labels_ref[...] = jnp.where(class_ref[...] == kinds, weight_ref[...], jnp.float32(0.0))
-    results = [
-        pltpu.make_async_copy(labels_ref, labels_hbm, small_sems.at[0])
-    ]
-    results[0].start()
-
-    def add(s, carry):
-        place = rows_ref[0, 0, s] * col_blocks + cols_ref[0, 0, s]
-        dense[place] += tiles[s].astype(jnp.float32)
-        return carry
-
-    for k in range(CHUNKS):
-        copies[k].wait()
-        lax.fori_loop(k * chunk, jnp.clip(count, k * chunk, (k + 1) * chunk), add, 0)
-
-    members = row_blocks // NB_DEV
-    col_sums = [jnp.zeros((8, side), jnp.float32) for _ in range(col_blocks)]
-    for r in range(row_blocks):
-        row_sum = jnp.zeros((side, side), jnp.float32)
-        for c in range(col_blocks):
-            block = dense[r * col_blocks + c]
-            w_ref[r * side : (r + 1) * side, c * side : (c + 1) * side] = block.astype(jnp.bfloat16)
-            row_sum = row_sum + block
-            col_sums[c] = col_sums[c] + jnp.sum(block.reshape(side // 8, 8, side), axis=0)
-        at = (r % NB_DEV) * side
-        sums_ref[r // NB_DEV, :, at : at + side] = jnp.sum(row_sum.T, axis=0, keepdims=True)
-        strip = pl.ds(r * side, side)
-        results.append(pltpu.make_async_copy(w_ref.at[strip], w_hbm.at[strip], out_sems.at[r]))
-        results[-1].start()
-    for c in range(col_blocks):
-        at = (c % NB_DEV) * side
-        sums_ref[members + c // NB_DEV, :, at : at + side] = jnp.sum(col_sums[c], axis=0, keepdims=True)
-    results.append(pltpu.make_async_copy(sums_ref, sums_hbm, small_sems.at[1]))
-    results[-1].start()
-    for copy in results:
-        copy.wait()
-
-
-def split(panel):
-    high = panel.astype(jnp.bfloat16)
-    low = (panel - high.astype(jnp.float32)).astype(jnp.bfloat16)
-    return jnp.concatenate([high, low], axis=0)
-
-
-def solve_kernel(
-    n_clu,
-    n_mem,
-    w_hbm,
-    sums_hbm,
-    labels_hbm,
-    scores_ref,
-    residual_ref,
-    w,
+    hot_rows,
+    hot_cols,
+    from_rows,
+    from_cols,
     sums_ref,
-    labels_ref,
     deg_m,
     deg_c,
     own,
@@ -217,6 +130,7 @@
     dots_m,
     dots_c,
     load_sems,
+    tile_sems,
     send_m,
     recv_m,
     send_c,
@@ -227,14 +141,27 @@
     others_m = [None] + [lax.rem(me_m + k, n_mem) for k in range(1, n_mem)]
     others_c = [None] + [lax.rem(me_c + k, n_clu) for k in range(1, n_clu)]
 
+    slots, side, _ = tiles.shape
+    row_blocks = NB_DEV * n_mem
+    col_blocks = NB_DEV * n_clu
+    steps = slots // GROUP
+
     loads = [
-        pltpu.make_async_copy(sums_hbm, sums_ref, load_sems.at[0]),
-        pltpu.make_async_copy(labels_hbm, labels_ref, load_sems.at[1]),
+        pltpu.make_async_copy(rows_hbm, rows_ref, load_sems.at[0]),
+        pltpu.make_async_copy(cols_hbm, cols_ref, load_sems.at[1]),
+        pltpu.make_async_copy(count_hbm, count_ref, load_sems.at[2]),
+        pltpu.make_async_copy(class_hbm, class_ref, load_sems.at[3]),
+        pltpu.make_async_copy(weight_hbm, weight_ref, load_sems.at[4]),
     ]
-    w_copy = pltpu.make_async_copy(w_hbm, w, load_sems.at[2])
+
+    def tile_copy(g):
+        part = pl.ds(g * GROUP, GROUP)
+        return pltpu.make_async_copy(tiles_hbm.at[0, 0, part], tiles.at[part], tile_sems.at[g])
+
     for copy in loads:
         copy.start()
-    w_copy.start()
+    for g in range(steps):
+        tile_copy(g).start()
     barrier = pltpu.get_barrier_semaphore()
     for k in range(1, n_mem):
         pl.semaphore_signal(barrier, device_id=(me_c, others_m[k]), device_id_type=MESH)
@@ -274,7 +201,86 @@
 
     for copy in loads:
         copy.wait()
-    labels = labels_ref[...]
+    count = count_ref[0, 0]
+    kinds = lax.broadcasted_iota(jnp.int32, (CLASSES, weight_ref.shape[1]), 0)
+    labels = jnp.where(class_ref[...] == kinds, weight_ref[...], jnp.float32(0.0))
+
+    for blocks, hot in ((row_blocks, hot_rows), (col_blocks, hot_cols)):
+        at = lax.broadcasted_iota(jnp.int32, (blocks, side), 0)
+        for k in range(blocks + 1):
+            hot[k] = jnp.where(at == k, jnp.float32(1.0), jnp.float32(0.0))
+    from_rows[...] = jnp.zeros_like(from_rows)
+    from_cols[...] = jnp.zeros_like(from_cols)
+
+    def used(slot, block, blocks):
+        unused = 1 - jnp.clip(count - slot, 0, 1)
+        return block + (blocks - block) * unused
+
+    def dot_rows(left, slot):
+        return lax.dot_general(
+            left, tiles[slot], (((1,), (1,)), ((), ())), preferred_element_type=jnp.float32
+        )
+
+    def dot_cols(left, slot):
+        right = tiles[pl.ds(slot, PACK)].reshape(PACK * side, side)
+        return lax.dot_general(
+            left, right, (((1,), (0,)), ((), ())), preferred_element_type=jnp.float32
+        )
+
+    def add_totals(g, carry):
+        row_total, col_total = carry
+        tile_copy(g).wait()
+        for k in range(0, GROUP, PACK):
+            packed = []
+            for slot in [g * GROUP + k + e for e in range(PACK)]:
+                row = used(slot, rows_ref[0, 0, slot], row_blocks)
+                col = used(slot, cols_ref[0, 0, slot], col_blocks)
+                row_total = row_total + dot_rows(hot_rows[row].astype(jnp.bfloat16), slot)
+                packed.append(hot_cols[col].astype(jnp.bfloat16))
+            col_total = col_total + dot_cols(jnp.concatenate(packed, axis=1), g * GROUP + k)
+        return row_total, col_total
+
+    row_total, col_total = lax.fori_loop(
+        0,
+        steps,
+        add_totals,
+        (jnp.zeros((row_blocks, side), jnp.float32), jnp.zeros((col_blocks, side), jnp.float32)),
+    )
+    for k in range(row_blocks):
+        at = k % NB_DEV * side
+        sums_ref[k // NB_DEV, :, at : at + side] = row_total[k : k + 1]
+    for k in range(col_blocks):
+        at = k % NB_DEV * side
+        sums_ref[n_mem + k // NB_DEV, :, at : at + side] = col_total[k : k + 1]
+
+    def column_sums():
+        def step(g, total):
+            for k in range(0, GROUP, PACK):
+                packed = []
+                for slot in [g * GROUP + k + e for e in range(PACK)]:
+                    row = used(slot, rows_ref[0, 0, slot], row_blocks)
+                    start = col_blocks - 1 - cols_ref[0, 0, slot]
+                    left = from_rows[row, pl.ds(start, col_blocks)]
+                    packed.append(left.reshape(col_blocks * CLASSES, side).astype(jnp.bfloat16))
+                total = total + dot_cols(jnp.concatenate(packed, axis=1), g * GROUP + k)
+            return total
+
+        zero = jnp.zeros((col_blocks * CLASSES, side), jnp.float32)
+        return lax.fori_loop(0, steps, step, zero)
+
+    def row_sums():
+        def step(g, total):
+            for slot in [g * GROUP + k for k in range(GROUP)]:
+                col = used(slot, cols_ref[0, 0, slot], col_blocks)
+                start = row_blocks - 1 - rows_ref[0, 0, slot]
+                left = from_cols[col, pl.ds(start, row_blocks)]
+                left = left.reshape(row_blocks * CLASSES, side).astype(jnp.bfloat16)
+                total = total + dot_rows(left, slot)
+            return total
+
+        zero = jnp.zeros((row_blocks * CLASSES, side), jnp.float32)
+        return lax.fori_loop(0, steps, step, zero)
+
     pl.semaphore_wait(barrier, n_mem + n_clu - 2)
 
     from_m = over_mem(0, lambda o: sums_ref.at[o], lambda k: deg_m.at[k], deg_m)
@@ -296,30 +302,35 @@
         from_c = over_clu(1 + 2 * step, lambda o: own.at[step], lambda k: pan_c.at[step, me_c], pan_c.at[step])
         return from_m, from_c
 
-    def multiply(step, from_m, from_c, prepare, between):
+    def blocks_of(panels):
+        for owner, panel in enumerate(panels):
+            for k in range(NB_DEV):
+                yield owner * NB_DEV + k, panel[:, k * side : (k + 1) * side]
+
+    def multiply(step, from_m, from_c, between):
         phase = 2 + 2 * step
         from_m.wait()
-        left = jnp.concatenate([pan_m[step, k] for k in range(n_mem)], axis=1)
-        if step == 0:
-            w_copy.wait()
-        out = lax.dot_general(
-            prepare(left), w[...], (((1,), (0,)), ((), ())), preferred_element_type=jnp.float32
-        )
-        out = out[:CLASSES] if step == 0 else out[:CLASSES] + out[CLASSES:]
-        width = out.shape[1] // n_clu
-        for k in range(n_clu):
-            part_c[step, k] = out[:, k * width : (k + 1) * width]
-        back_c = over_clu(phase, lambda o: part_c.at[step, o], lambda k: got_c.at[step, k], got_c.at[step])
+        for k, block in blocks_of([pan_m[step, k] for k in range(n_mem)]):
+            from_rows[k, col_blocks - 1] = block
+        out = column_sums()
+        for k in range(col_blocks):
+            at = k % NB_DEV * side
+            part_c[step, k // NB_DEV, :, at : at + side] = out[k * CLASSES : (k + 1) * CLASSES]
+        back_c = over_clu(
+            phase, lambda o: part_c.at[step, o], lambda k: got_c.at[step, k], got_c.at[step]
+        )
         from_c.wait()
-        right = jnp.concatenate([pan_c[step, k] for k in range(n_clu)], axis=1)
-        between(right, out)
-        out = lax.dot_general(
-            prepare(right), w[...], (((1,), (1,)), ((), ())), preferred_element_type=jnp.float32
-        )
-        out = out[:CLASSES] if step == 0 else out[:CLASSES] + out[CLASSES:]
-        for k in range(n_mem):
-            part_m[step, k] = out[:, k * width : (k + 1) * width]
-        back_m = over_mem(phase, lambda o: part_m.at[step, o], lambda k: got_m.at[step, k], got_m.at[step])
+        panels = [pan_c[step, k] for k in range(n_clu)]
+        for k, block in blocks_of(panels):
+            from_cols[k, row_blocks - 1] = block
+        between(panels)
+        out = row_sums()
+        for k in range(row_blocks):
+            at = k % NB_DEV * side
+            part_m[step, k // NB_DEV, :, at : at + side] = out[k * CLASSES : (k + 1) * CLASSES]
+        back_m = over_mem(
+            phase, lambda o: part_m.at[step, o], lambda k: got_m.at[step, k], got_m.at[step]
+        )
         return back_m, back_c
 
     def collect(step, back_m, back_c):
@@ -333,9 +344,7 @@
         return 0.99 * root * image
 
     from_m, from_c = gather(0, root * labels)
-    back_m, back_c = multiply(
-        0, from_m, from_c, lambda x: x.astype(jnp.bfloat16), lambda right, out: None
-    )
+    back_m, back_c = multiply(0, from_m, from_c, lambda panels: None)
     first = collect(0, back_m, back_c)
 
     from_m, from_c = gather(1, root * first)
@@ -348,15 +357,18 @@
     ]
     dot_copies = []
 
-    def send_sums(right, image):
-        cross = 1.98 * jnp.sum(right * image, axis=1, keepdims=True)
+    def send_sums(panels):
+        cross = panels[0] * part_c[1, 0]
+        for k in range(1, n_clu):
+            cross = cross + panels[k] * part_c[1, k]
+        cross = 1.98 * jnp.sum(cross, axis=1, keepdims=True)
         line = jnp.zeros((CLASSES, 128), jnp.float32)
         for k, value in enumerate([*sums, cross]):
             line = line + jnp.where(lane == kind + k * CLASSES, value, 0.0)
         dots[0] = jnp.sum(line, axis=0, keepdims=True)
         dot_copies.append(over_mem(5, lambda o: dots.at[0], lambda k: dots_m.at[k], dots_m))
 
-    back_m, back_c = multiply(1, from_m, from_c, split, send_sums)
+    back_m, back_c = multiply(1, from_m, from_c, send_sums)
     dot_copies[0].wait()
     line = dots[0]
     for k in range(1, n_mem):
@@ -401,55 +413,36 @@
         copy.wait()
 
 
-def on_device_dense(seed_class, seed_weight, tile_values, tile_rows, tile_cols, tile_count):
+def on_device_kernel(seed_class, seed_weight, tile_values, tile_rows, tile_cols, tile_count):
     n_clu = lax.axis_size("clu")
     n_mem = lax.axis_size("mem")
     _, _, slots, side, _ = tile_values.shape
     nodes = NB_DEV * side
-    rows = nodes * n_mem
-    cols = nodes * n_clu
+    row_blocks = NB_DEV * n_mem
+    col_blocks = NB_DEV * n_clu
     f32 = jnp.float32
+    hbm = pl.BlockSpec(memory_space=pltpu.HBM)
     vmem = pl.BlockSpec(memory_space=pltpu.VMEM)
-    hbm = pl.BlockSpec(memory_space=pltpu.HBM)
+    dma = pltpu.SemaphoreType.DMA
     panel = (CLASSES, nodes)
-    w, sums, labels = pl.pallas_call(
-        densify_kernel,
-        out_shape=(
-            jax.ShapeDtypeStruct((rows, cols), jnp.bfloat16),
-            jax.ShapeDtypeStruct((n_mem + n_clu, 1, nodes), f32),
-            jax.ShapeDtypeStruct(panel, f32),
-        ),
+    results = (jax.ShapeDtypeStruct(panel, f32), jax.ShapeDtypeStruct(panel, f32))
+    found = pl.pallas_call(
+        functools.partial(solve_kernel, n_clu, n_mem),
+        out_shape=results,
         in_specs=[hbm] * 6,
-        out_specs=(hbm, hbm, hbm),
+        out_specs=(vmem, vmem),
         scratch_shapes=[
-            pltpu.VMEM((rows, cols), jnp.bfloat16),
-            pltpu.VMEM((n_mem + n_clu, 1, nodes), f32),
-            pltpu.VMEM(panel, f32),
             pltpu.VMEM((1, nodes), jnp.int32),
             pltpu.VMEM((1, nodes), f32),
             pltpu.SMEM(tile_rows.shape, jnp.int32),
             pltpu.SMEM(tile_cols.shape, jnp.int32),
             pltpu.SMEM(tile_count.shape, jnp.int32),
             pltpu.VMEM((slots, side, side), tile_values.dtype),
-            pltpu.VMEM((rows * cols // (side * side), side, side), f32),
-            pltpu.SemaphoreType.DMA((5,)),
-            pltpu.SemaphoreType.DMA((CHUNKS,)),
-            pltpu.SemaphoreType.DMA((rows // side,)),
-        ],
-        compiler_params=pltpu.CompilerParams(vmem_limit_bytes=VMEM_LIMIT),
-        name="densify",
-    )(tile_rows, tile_cols, tile_count, tile_values, seed_class[None], seed_weight[None])
-    dma = pltpu.SemaphoreType.DMA
-    results = (jax.ShapeDtypeStruct(panel, f32), jax.ShapeDtypeStruct(panel, f32))
-    found = pl.pallas_call(
-        functools.partial(solve_kernel, n_clu, n_mem),
-        out_shape=results,
-        in_specs=[hbm] * 3,
-        out_specs=(vmem, vmem),
-        scratch_shapes=[
-            pltpu.VMEM((rows, cols), jnp.bfloat16),
+            pltpu.VMEM((row_blocks + 1, row_blocks, side), f32),
+            pltpu.VMEM((col_blocks + 1, col_blocks, side), f32),
+            pltpu.VMEM((row_blocks + 1, 2 * col_blocks - 1, CLASSES, side), f32),
+            pltpu.VMEM((col_blocks + 1, 2 * row_blocks - 1, CLASSES, side), f32),
             pltpu.VMEM((n_mem + n_clu, 1, nodes), f32),
-            pltpu.VMEM(panel, f32),
             pltpu.VMEM((n_mem, 1, nodes), f32),
             pltpu.VMEM((n_clu, 1, nodes), f32),
             pltpu.VMEM((ITERS, *panel), f32),
@@ -462,7 +455,8 @@
             pltpu.VMEM((2, 1, 128), f32),
             pltpu.VMEM((n_mem, 1, 128), f32),
             pltpu.VMEM((n_clu, 1, 128), f32),
-            dma((3,)),
+            dma((5,)),
+            dma((slots // GROUP,)),
             dma((2 + 2 * ITERS,)),
             dma((2 + 2 * ITERS,)),
             dma((2 + 2 * ITERS,)),
@@ -472,7 +466,7 @@
             collective_id=0, has_side_effects=True, vmem_limit_bytes=VMEM_LIMIT
         ),
         name="solve",
-    )(w, sums, labels)
+    )(seed_class[None], seed_weight[None], tile_values, tile_rows, tile_cols, tile_count)
     return pl.pallas_call(
         finish_kernel,
         out_shape=results,
@@ -487,8 +481,8 @@
 def on_device(seed_class, seed_weight, tile_values, tile_rows, tile_cols, tile_count):
     side = tile_values.shape[-1]
     blocks = NB_DEV * lax.axis_size("mem") * NB_DEV * lax.axis_size("clu")
-    if blocks * side * side * 4 <= DENSE_LIMIT:
-        run = on_device_dense
+    if blocks * CLASSES * side * 16 <= TABLE_LIMIT:
+        run = on_device_kernel
     else:
         run = on_device_slots
     return run(seed_class, seed_weight, tile_values, tile_rows, tile_cols, tile_count)

time: 38.4 us -> 40.2 us (1.047)
  Pallas kernels: 36.8 us -> 38.7 us
    pallas_call x3 -> x2, Pallas kernels: 36.8 us -> 38.7 us  [the longest x1 37.1 us: on_device_kernel(): pl.pallas_call(functools.partial(solve_kernel, n_clu, n_mem), out_shape=r...]
where the time goes in v4:
time: 40.2 us; the launch traced here: 40 us
  Pallas kernels  38.7 us (96%)
  between operations  1.29 us (3%)
    pallas_call x1, Pallas kernels, on_device_kernel(): pl.pallas_call(functools.partial(solve_kernel, n_clu, n_mem), out_shape=r...  37.1 us
    pallas_call x1, Pallas kernels, on_device_kernel(): pl.pallas_call(finish_kernel, out_shape=results, in_specs=[hbm, hbm], out...  1.62 us

profile of v4, /device:TPU:0, one launch (start us, length us, event | category | flops | bytes accessed | tf_op | source)
XLA Modules:
  0.0 40.0 jit_solution(15588396230921487858)
XLA Ops:
  1.3 37.1 %solve.1 = (f32[8,256]{1,0:T(8,128)}, f32[8,256]{1,0:T(8,128)}) custom-call(s32[1,256]{1,0:T(1,128)} %bitcast.2, f32[1,256]{1,0:T(1,128)} %bitcast.3, bf16[1,1,96,128,128]{4,3,2,1,0:T(8,128)(2,1)} %tiles_hbm.1, s32[1,1,96]{2,1,0:T(1,128)} %rows_hbm.1, s32[1,1,96]{2,1,0:T(1,128)} %cols_hbm.1, s32[1,1]{1,0:T(1,128)S(6)} %copy.8.count_hbm), custom_call_target="tpu_custom_call" | custom-call | tf_op jit(solution)/shard_map/solve/pallas_call | solution.py:429
  38.4 1.6 %finish.1 = (f32[8,256]{1,0:T(8,128)}, f32[8,256]{1,0:T(8,128)}) custom-call(f32[8,256]{1,0:T(8,128)} %get-tuple-element.4.scores_in, f32[8,256]{1,0:T(8,128)} %get-tuple-element.5.residual_in), custom_call_target="tpu_custom_call" | custom-call | tf_op jit(solution)/shard_map/finish/pallas_call | solution.py:470

commit v5 on v4

--- a/solution.py
+++ b/solution.py
@@ -10,6 +10,7 @@
 NB_DEV = 2
 ITERS = 2
 GROUP = 16
+SPAN = 48
 PACK = 4
 TABLE_LIMIT = 16 * 1024 * 1024
 VMEM_LIMIT = 64 * 1024 * 1024
@@ -112,6 +113,7 @@
     cols_ref,
     count_ref,
     tiles,
+    turned,
     hot_rows,
     hot_cols,
     from_rows,
@@ -216,28 +218,35 @@
         unused = 1 - jnp.clip(count - slot, 0, 1)
         return block + (blocks - block) * unused
 
-    def dot_rows(left, slot):
+    def dot(left, held, slot):
+        right = held[pl.ds(slot, PACK)].reshape(PACK * side, side)
         return lax.dot_general(
-            left, tiles[slot], (((1,), (1,)), ((), ())), preferred_element_type=jnp.float32
-        )
-
-    def dot_cols(left, slot):
-        right = tiles[pl.ds(slot, PACK)].reshape(PACK * side, side)
-        return lax.dot_general(
-            left, right, (((1,), (0,)), ((), ())), preferred_element_type=jnp.float32
+            jnp.concatenate(left, axis=1),
+            right,
+            (((1,), (0,)), ((), ())),
+            preferred_element_type=jnp.float32,
         )
 
     def add_totals(g, carry):
         row_total, col_total = carry
         tile_copy(g).wait()
         for k in range(0, GROUP, PACK):
-            packed = []
-            for slot in [g * GROUP + k + e for e in range(PACK)]:
+            first = g * GROUP + k
+            by_row, by_col = [], []
+            for slot in [first + e for e in range(PACK)]:
                 row = used(slot, rows_ref[0, 0, slot], row_blocks)
                 col = used(slot, cols_ref[0, 0, slot], col_blocks)
-                row_total = row_total + dot_rows(hot_rows[row].astype(jnp.bfloat16), slot)
-                packed.append(hot_cols[col].astype(jnp.bfloat16))
-            col_total = col_total + dot_cols(jnp.concatenate(packed, axis=1), g * GROUP + k)
+                by_row.append(hot_rows[row].astype(jnp.bfloat16))
+                by_col.append(hot_cols[col].astype(jnp.bfloat16))
+            col_total = col_total + dot(by_col, tiles, first)
+            for e in range(0, PACK, 2):
+                pair = lax.dot_general(
+                    jnp.concatenate(by_row[e : e + 2], axis=0),
+                    tiles[pl.ds(first + e, 2)].reshape(2 * side, side),
+                    (((1,), (1,)), ((), ())),
+                    preferred_element_type=jnp.float32,
+                )
+                row_total = row_total + pair[:row_blocks, :side] + pair[row_blocks:, side:]
         return row_total, col_total
 
     row_total, col_total = lax.fori_loop(
@@ -253,38 +262,37 @@
         at = k % NB_DEV * side
         sums_ref[n_mem + k // NB_DEV, :, at : at + side] = col_total[k : k + 1]
 
+    def turn(g, carry):
+        for slot in [g * GROUP + k for k in range(GROUP)]:
+            turned[slot] = tiles[slot].T
+        return carry
+
+    def place_sums(table, held, own_ref, own_blocks, to_ref, to_blocks):
+        def step(g, total):
+            for k in range(0, SPAN, PACK):
+                left = []
+                for slot in [g * SPAN + k + e for e in range(PACK)]:
+                    block = used(slot, own_ref[0, 0, slot], own_blocks)
+                    start = to_blocks - 1 - to_ref[0, 0, slot]
+                    panel = table[block, pl.ds(start, to_blocks)]
+                    left.append(panel.reshape(to_blocks * CLASSES, side).astype(jnp.bfloat16))
+                total = total + dot(left, held, g * SPAN + k)
+            return total
+
+        zero = jnp.zeros((to_blocks * CLASSES, side), jnp.float32)
+        return lax.fori_loop(0, slots // SPAN, step, zero)
+
     def column_sums():
-        def step(g, total):
-            for k in range(0, GROUP, PACK):
-                packed = []
-                for slot in [g * GROUP + k + e for e in range(PACK)]:
-                    row = used(slot, rows_ref[0, 0, slot], row_blocks)
-                    start = col_blocks - 1 - cols_ref[0, 0, slot]
-                    left = from_rows[row, pl.ds(start, col_blocks)]
-                    packed.append(left.reshape(col_blocks * CLASSES, side).astype(jnp.bfloat16))
-                total = total + dot_cols(jnp.concatenate(packed, axis=1), g * GROUP + k)
-            return total
-
-        zero = jnp.zeros((col_blocks * CLASSES, side), jnp.float32)
-        return lax.fori_loop(0, steps, step, zero)
+        return place_sums(from_rows, tiles, rows_ref, row_blocks, cols_ref, col_blocks)
 
     def row_sums():
-        def step(g, total):
-            for slot in [g * GROUP + k for k in range(GROUP)]:
-                col = used(slot, cols_ref[0, 0, slot], col_blocks)
-                start = row_blocks - 1 - rows_ref[0, 0, slot]
-                left = from_cols[col, pl.ds(start, row_blocks)]
-                left = left.reshape(row_blocks * CLASSES, side).astype(jnp.bfloat16)
-                total = total + dot_rows(left, slot)
-            return total
-
-        zero = jnp.zeros((row_blocks * CLASSES, side), jnp.float32)
-        return lax.fori_loop(0, steps, step, zero)
+        return place_sums(from_cols, turned, cols_ref, col_blocks, rows_ref, row_blocks)
 
     pl.semaphore_wait(barrier, n_mem + n_clu - 2)
 
     from_m = over_mem(0, lambda o: sums_ref.at[o], lambda k: deg_m.at[k], deg_m)
     from_c = over_clu(0, lambda o: sums_ref.at[n_mem + o], lambda k: deg_c.at[k], deg_c)
+    lax.fori_loop(0, steps, turn, 0)
     degree = 1.0 + (sums_ref[me_m] + sums_ref[n_mem + me_c])
     from_m.wait()
     for k in range(1, n_mem):
@@ -437,6 +445,7 @@
             pltpu.SMEM(tile_rows.shape, jnp.int32),
             pltpu.SMEM(tile_cols.shape, jnp.int32),
             pltpu.SMEM(tile_count.shape, jnp.int32),
+            pltpu.VMEM((slots, side, side), tile_values.dtype),
             pltpu.VMEM((slots, side, side), tile_values.dtype),
             pltpu.VMEM((row_blocks + 1, row_blocks, side), f32),
             pltpu.VMEM((col_blocks + 1, col_blocks, side), f32),

time: 40.2 us -> 36.3 us (0.903)
  Pallas kernels: 38.7 us -> 34.8 us
    pallas_call x1, Pallas kernels: 37.1 us -> 33.2 us  [on_device_kernel(): pl.pallas_call(functools.partial(solve_kernel, n_clu, n_mem), out_shape=r...]
where the time goes in v5:
time: 36.3 us; the launch traced here: 36.1 us
  Pallas kernels  34.8 us (96%)
  between operations  1.29 us (4%)
    pallas_call x1, Pallas kernels, on_device_kernel(): pl.pallas_call(functools.partial(solve_kernel, n_clu, n_mem), out_shape=r...  33.2 us
    pallas_call x1, Pallas kernels, on_device_kernel(): pl.pallas_call(finish_kernel, out_shape=results, in_specs=[hbm, hbm], out...  1.62 us

profile of v5, /device:TPU:0, one launch (start us, length us, event | category | flops | bytes accessed | tf_op | source)
XLA Modules:
  0.0 36.1 jit_solution(16715891616880973363)
XLA Ops:
  1.3 33.2 %solve.1 = (f32[8,256]{1,0:T(8,128)}, f32[8,256]{1,0:T(8,128)}) custom-call(s32[1,256]{1,0:T(1,128)} %bitcast.2, f32[1,256]{1,0:T(1,128)} %bitcast.3, bf16[1,1,96,128,128]{4,3,2,1,0:T(8,128)(2,1)} %tiles_hbm.1, s32[1,1,96]{2,1,0:T(1,128)} %rows_hbm.1, s32[1,1,96]{2,1,0:T(1,128)} %cols_hbm.1, s32[1,1]{1,0:T(1,128)S(6)} %copy.8.count_hbm), custom_call_target="tpu_custom_call" | custom-call | tf_op jit(solution)/shard_map/solve/pallas_call | solution.py:437
  34.5 1.6 %finish.1 = (f32[8,256]{1,0:T(8,128)}, f32[8,256]{1,0:T(8,128)}) custom-call(f32[8,256]{1,0:T(8,128)} %get-tuple-element.4.scores_in, f32[8,256]{1,0:T(8,128)} %get-tuple-element.5.residual_in), custom_call_target="tpu_custom_call" | custom-call | tf_op jit(solution)/shard_map/finish/pallas_call | solution.py:479

commit v6 on v5

--- a/solution.py
+++ b/solution.py
@@ -10,7 +10,7 @@
 NB_DEV = 2
 ITERS = 2
 GROUP = 16
-SPAN = 48
+SPAN = 96
 PACK = 4
 TABLE_LIMIT = 16 * 1024 * 1024
 VMEM_LIMIT = 64 * 1024 * 1024
@@ -292,7 +292,7 @@
 
     from_m = over_mem(0, lambda o: sums_ref.at[o], lambda k: deg_m.at[k], deg_m)
     from_c = over_clu(0, lambda o: sums_ref.at[n_mem + o], lambda k: deg_c.at[k], deg_c)
-    lax.fori_loop(0, steps, turn, 0)
+    lax.fori_loop(0, steps // 2, turn, 0)
     degree = 1.0 + (sums_ref[me_m] + sums_ref[n_mem + me_c])
     from_m.wait()
     for k in range(1, n_mem):
@@ -303,6 +303,9 @@
     root = lax.rsqrt(degree)
 
     def gather(step, panel):
+        panel = jnp.concatenate(
+            [panel[:, k * side : (k + 1) * side] for k in range(NB_DEV)], axis=0
+        ).astype(jnp.bfloat16)
         own[step] = panel
         pan_m[step, me_m] = panel
         pan_c[step, me_c] = panel
@@ -310,16 +313,13 @@
         from_c = over_clu(1 + 2 * step, lambda o: own.at[step], lambda k: pan_c.at[step, me_c], pan_c.at[step])
         return from_m, from_c
 
-    def blocks_of(panels):
-        for owner, panel in enumerate(panels):
-            for k in range(NB_DEV):
-                yield owner * NB_DEV + k, panel[:, k * side : (k + 1) * side]
-
     def multiply(step, from_m, from_c, between):
         phase = 2 + 2 * step
         from_m.wait()
-        for k, block in blocks_of([pan_m[step, k] for k in range(n_mem)]):
-            from_rows[k, col_blocks - 1] = block
+        for k in range(n_mem):
+            panel = pan_m[step, k].astype(jnp.float32).reshape(NB_DEV, CLASSES, side)
+            for e in range(NB_DEV):
+                from_rows[k * NB_DEV + e, col_blocks - 1] = panel[e]
         out = column_sums()
         for k in range(col_blocks):
             at = k % NB_DEV * side
@@ -328,10 +328,13 @@
             phase, lambda o: part_c.at[step, o], lambda k: got_c.at[step, k], got_c.at[step]
         )
         from_c.wait()
-        panels = [pan_c[step, k] for k in range(n_clu)]
-        for k, block in blocks_of(panels):
-            from_cols[k, row_blocks - 1] = block
-        between(panels)
+        blocks = []
+        for k in range(n_clu):
+            panel = pan_c[step, k].astype(jnp.float32).reshape(NB_DEV, CLASSES, side)
+            for e in range(NB_DEV):
+                blocks.append(panel[e])
+                from_cols[k * NB_DEV + e, row_blocks - 1] = panel[e]
+        between(blocks, out)
         out = row_sums()
         for k in range(row_blocks):
             at = k % NB_DEV * side
@@ -352,7 +355,8 @@
         return 0.99 * root * image
 
     from_m, from_c = gather(0, root * labels)
-    back_m, back_c = multiply(0, from_m, from_c, lambda panels: None)
+    lax.fori_loop(steps // 2, steps, turn, 0)
+    back_m, back_c = multiply(0, from_m, from_c, lambda blocks, out: None)
     first = collect(0, back_m, back_c)
 
     from_m, from_c = gather(1, root * first)
@@ -365,10 +369,10 @@
     ]
     dot_copies = []
 
-    def send_sums(panels):
-        cross = panels[0] * part_c[1, 0]
-        for k in range(1, n_clu):
-            cross = cross + panels[k] * part_c[1, k]
+    def send_sums(blocks, out):
+        cross = jnp.zeros((CLASSES, side), jnp.float32)
+        for k, block in enumerate(blocks):
+            cross = cross + block * out[k * CLASSES : (k + 1) * CLASSES]
         cross = 1.98 * jnp.sum(cross, axis=1, keepdims=True)
         line = jnp.zeros((CLASSES, 128), jnp.float32)
         for k, value in enumerate([*sums, cross]):
@@ -433,6 +437,7 @@
     vmem = pl.BlockSpec(memory_space=pltpu.VMEM)
     dma = pltpu.SemaphoreType.DMA
     panel = (CLASSES, nodes)
+    sent = (NB_DEV * CLASSES, side)
     results = (jax.ShapeDtypeStruct(panel, f32), jax.ShapeDtypeStruct(panel, f32))
     found = pl.pallas_call(
         functools.partial(solve_kernel, n_clu, n_mem),
@@ -454,9 +459,9 @@
             pltpu.VMEM((n_mem + n_clu, 1, nodes), f32),
             pltpu.VMEM((n_mem, 1, nodes), f32),
             pltpu.VMEM((n_clu, 1, nodes), f32),
-            pltpu.VMEM((ITERS, *panel), f32),
-            pltpu.VMEM((ITERS, n_mem, *panel), f32),
-            pltpu.VMEM((ITERS, n_clu, *panel), f32),
+            pltpu.VMEM((ITERS, *sent), jnp.bfloat16),
+            pltpu.VMEM((ITERS, n_mem, *sent), jnp.bfloat16),
+            pltpu.VMEM((ITERS, n_clu, *sent), jnp.bfloat16),
             pltpu.VMEM((ITERS, n_mem, *panel), f32),
             pltpu.VMEM((ITERS, n_clu, *panel), f32),
             pltpu.VMEM((ITERS, n_mem, *panel), f32),

time: 36.3 us -> 35.5 us (0.978)
  Pallas kernels: 34.8 us -> 34.1 us
    pallas_call x1, Pallas kernels: 33.2 us -> 32.5 us  [on_device_kernel(): pl.pallas_call(functools.partial(solve_kernel, n_clu, n_mem), out_shape=r...]
where the time goes in v6:
time: 35.5 us; the launch traced here: 35.4 us
  Pallas kernels  34.1 us (96%)
  between operations  1.29 us (4%)
    pallas_call x1, Pallas kernels, on_device_kernel(): pl.pallas_call(functools.partial(solve_kernel, n_clu, n_mem), out_shape=r...  32.5 us
    pallas_call x1, Pallas kernels, on_device_kernel(): pl.pallas_call(finish_kernel, out_shape=results, in_specs=[hbm, hbm], out...  1.62 us

profile of v6, /device:TPU:0, one launch (start us, length us, event | category | flops | bytes accessed | tf_op | source)
XLA Modules:
  0.0 35.4 jit_solution(15326111816897503532)
XLA Ops:
  1.3 32.5 %solve.1 = (f32[8,256]{1,0:T(8,128)}, f32[8,256]{1,0:T(8,128)}) custom-call(s32[1,256]{1,0:T(1,128)} %bitcast.2, f32[1,256]{1,0:T(1,128)} %bitcast.3, bf16[1,1,96,128,128]{4,3,2,1,0:T(8,128)(2,1)} %tiles_hbm.1, s32[1,1,96]{2,1,0:T(1,128)} %rows_hbm.1, s32[1,1,96]{2,1,0:T(1,128)} %cols_hbm.1, s32[1,1]{1,0:T(1,128)S(6)} %copy.8.count_hbm), custom_call_target="tpu_custom_call" | custom-call | tf_op jit(solution)/shard_map/solve/pallas_call | solution.py:442
  33.7 1.6 %finish.1 = (f32[8,256]{1,0:T(8,128)}, f32[8,256]{1,0:T(8,128)}) custom-call(f32[8,256]{1,0:T(8,128)} %get-tuple-element.4.scores_in, f32[8,256]{1,0:T(8,128)} %get-tuple-element.5.residual_in), custom_call_target="tpu_custom_call" | custom-call | tf_op jit(solution)/shard_map/finish/pallas_call | solution.py:484

commit v7 on v6

--- a/solution.py
+++ b/solution.py
@@ -313,45 +313,45 @@
         from_c = over_clu(1 + 2 * step, lambda o: own.at[step], lambda k: pan_c.at[step, me_c], pan_c.at[step])
         return from_m, from_c
 
+    def place_panels(panels, count, table, at):
+        blocks = []
+        for k in range(count):
+            panel = panels[k].astype(jnp.float32).reshape(NB_DEV, CLASSES, side)
+            for e in range(NB_DEV):
+                blocks.append(panel[e])
+                table[k * NB_DEV + e, at] = panel[e]
+        return blocks
+
+    def parts_of(out, parts, blocks):
+        for k in range(blocks):
+            at = k % NB_DEV * side
+            parts[k // NB_DEV, :, at : at + side] = out[k * CLASSES : (k + 1) * CLASSES]
+
     def multiply(step, from_m, from_c, between):
         phase = 2 + 2 * step
+        from_c.wait()
+        place_panels(pan_c.at[step], n_clu, from_cols, row_blocks - 1)
+        out = row_sums()
+        parts_of(out, part_m.at[step], row_blocks)
+        back_m = over_mem(
+            phase, lambda o: part_m.at[step, o], lambda k: got_m.at[step, k], got_m.at[step]
+        )
         from_m.wait()
-        for k in range(n_mem):
-            panel = pan_m[step, k].astype(jnp.float32).reshape(NB_DEV, CLASSES, side)
-            for e in range(NB_DEV):
-                from_rows[k * NB_DEV + e, col_blocks - 1] = panel[e]
-        out = column_sums()
-        for k in range(col_blocks):
-            at = k % NB_DEV * side
-            part_c[step, k // NB_DEV, :, at : at + side] = out[k * CLASSES : (k + 1) * CLASSES]
+        between(place_panels(pan_m.at[step], n_mem, from_rows, col_blocks - 1), out)
+        parts_of(column_sums(), part_c.at[step], col_blocks)
         back_c = over_clu(
             phase, lambda o: part_c.at[step, o], lambda k: got_c.at[step, k], got_c.at[step]
         )
-        from_c.wait()
-        blocks = []
-        for k in range(n_clu):
-            panel = pan_c[step, k].astype(jnp.float32).reshape(NB_DEV, CLASSES, side)
-            for e in range(NB_DEV):
-                blocks.append(panel[e])
-                from_cols[k * NB_DEV + e, row_blocks - 1] = panel[e]
-        between(blocks, out)
-        out = row_sums()
-        for k in range(row_blocks):
-            at = k % NB_DEV * side
-            part_m[step, k // NB_DEV, :, at : at + side] = out[k * CLASSES : (k + 1) * CLASSES]
-        back_m = over_mem(
-            phase, lambda o: part_m.at[step, o], lambda k: got_m.at[step, k], got_m.at[step]
-        )
         return back_m, back_c
 
     def collect(step, back_m, back_c):
         image = part_m[step, me_m] + part_c[step, me_c]
+        back_m.wait()
+        for k in range(1, n_mem):
+            image = image + got_m[step, k]
         back_c.wait()
         for k in range(1, n_clu):
             image = image + got_c[step, k]
-        back_m.wait()
-        for k in range(1, n_mem):
-            image = image + got_m[step, k]
         return 0.99 * root * image
 
     from_m, from_c = gather(0, root * labels)
@@ -378,19 +378,19 @@
         for k, value in enumerate([*sums, cross]):
             line = line + jnp.where(lane == kind + k * CLASSES, value, 0.0)
         dots[0] = jnp.sum(line, axis=0, keepdims=True)
-        dot_copies.append(over_mem(5, lambda o: dots.at[0], lambda k: dots_m.at[k], dots_m))
+        dot_copies.append(over_clu(5, lambda o: dots.at[0], lambda k: dots_c.at[k], dots_c))
 
     back_m, back_c = multiply(1, from_m, from_c, send_sums)
     dot_copies[0].wait()
     line = dots[0]
+    for k in range(1, n_clu):
+        line = line + dots_c[k]
+    dots[1] = line
+    dot_copies.append(over_mem(5, lambda o: dots.at[1], lambda k: dots_m.at[k], dots_m))
+    second = collect(1, back_m, back_c)
+    dot_copies[1].wait()
     for k in range(1, n_mem):
         line = line + dots_m[k]
-    dots[1] = line
-    dot_copies.append(over_clu(5, lambda o: dots.at[1], lambda k: dots_c.at[k], dots_c))
-    second = collect(1, back_m, back_c)
-    dot_copies[1].wait()
-    for k in range(1, n_clu):
-        line = line + dots_c[k]
     spread_line = jnp.broadcast_to(line, (CLASSES, 128))
     bb, bq, qq, qt = [
         jnp.sum(

time: 35.5 us -> 33.6 us (0.946)
  Pallas kernels: 34.1 us -> 32.1 us
    pallas_call x1, Pallas kernels: 32.5 us -> 30.5 us  [on_device_kernel(): pl.pallas_call(functools.partial(solve_kernel, n_clu, n_mem), out_shape=r...]
where the time goes in v7:
time: 33.6 us; the launch traced here: 33.4 us
  Pallas kernels  32.1 us (96%)
  between operations  1.29 us (4%)
    pallas_call x1, Pallas kernels, on_device_kernel(): pl.pallas_call(functools.partial(solve_kernel, n_clu, n_mem), out_shape=r...  30.5 us
    pallas_call x1, Pallas kernels, on_device_kernel(): pl.pallas_call(finish_kernel, out_shape=results, in_specs=[hbm, hbm], out...  1.62 us

profile of v7, /device:TPU:0, one launch (start us, length us, event | category | flops | bytes accessed | tf_op | source)
XLA Modules:
  0.0 33.4 jit_solution(16228116800712689986)
XLA Ops:
  1.3 30.5 %solve.1 = (f32[8,256]{1,0:T(8,128)}, f32[8,256]{1,0:T(8,128)}) custom-call(s32[1,256]{1,0:T(1,128)} %bitcast.2, f32[1,256]{1,0:T(1,128)} %bitcast.3, bf16[1,1,96,128,128]{4,3,2,1,0:T(8,128)(2,1)} %tiles_hbm.1, s32[1,1,96]{2,1,0:T(1,128)} %rows_hbm.1, s32[1,1,96]{2,1,0:T(1,128)} %cols_hbm.1, s32[1,1]{1,0:T(1,128)S(6)} %copy.8.count_hbm), custom_call_target="tpu_custom_call" | custom-call | tf_op jit(solution)/shard_map/solve/pallas_call | solution.py:442
  31.8 1.6 %finish.1 = (f32[8,256]{1,0:T(8,128)}, f32[8,256]{1,0:T(8,128)}) custom-call(f32[8,256]{1,0:T(8,128)} %get-tuple-element.4.scores_in, f32[8,256]{1,0:T(8,128)} %get-tuple-element.5.residual_in), custom_call_target="tpu_custom_call" | custom-call | tf_op jit(solution)/shard_map/finish/pallas_call | solution.py:484

commit v8 on v7

--- a/solution.py
+++ b/solution.py
@@ -227,40 +227,36 @@
             preferred_element_type=jnp.float32,
         )
 
-    def add_totals(g, carry):
-        row_total, col_total = carry
+    def blocks_used(first, count, own_ref, own_blocks, hot):
+        return [
+            hot[used(slot, own_ref[0, 0, slot], own_blocks)].astype(jnp.bfloat16)
+            for slot in range(first, first + count)
+        ]
+
+    total = jnp.zeros((row_blocks, side), jnp.float32)
+    for g in range(steps):
         tile_copy(g).wait()
-        for k in range(0, GROUP, PACK):
-            first = g * GROUP + k
-            by_row, by_col = [], []
-            for slot in [first + e for e in range(PACK)]:
-                row = used(slot, rows_ref[0, 0, slot], row_blocks)
-                col = used(slot, cols_ref[0, 0, slot], col_blocks)
-                by_row.append(hot_rows[row].astype(jnp.bfloat16))
-                by_col.append(hot_cols[col].astype(jnp.bfloat16))
-            col_total = col_total + dot(by_col, tiles, first)
-            for e in range(0, PACK, 2):
-                pair = lax.dot_general(
-                    jnp.concatenate(by_row[e : e + 2], axis=0),
-                    tiles[pl.ds(first + e, 2)].reshape(2 * side, side),
-                    (((1,), (1,)), ((), ())),
-                    preferred_element_type=jnp.float32,
-                )
-                row_total = row_total + pair[:row_blocks, :side] + pair[row_blocks:, side:]
-        return row_total, col_total
-
-    row_total, col_total = lax.fori_loop(
-        0,
-        steps,
-        add_totals,
-        (jnp.zeros((row_blocks, side), jnp.float32), jnp.zeros((col_blocks, side), jnp.float32)),
-    )
+        for first in range(g * GROUP, (g + 1) * GROUP, 2):
+            pair = lax.dot_general(
+                jnp.concatenate(blocks_used(first, 2, rows_ref, row_blocks, hot_rows), axis=0),
+                tiles[pl.ds(first, 2)].reshape(2 * side, side),
+                (((1,), (1,)), ((), ())),
+                preferred_element_type=jnp.float32,
+            )
+            total = total + pair[:row_blocks, :side] + pair[row_blocks:, side:]
     for k in range(row_blocks):
         at = k % NB_DEV * side
-        sums_ref[k // NB_DEV, :, at : at + side] = row_total[k : k + 1]
+        sums_ref[k // NB_DEV, :, at : at + side] = total[k : k + 1]
+    pl.semaphore_wait(barrier, n_mem + n_clu - 2)
+    from_m = over_mem(0, lambda o: sums_ref.at[o], lambda k: deg_m.at[k], deg_m)
+
+    total = jnp.zeros((col_blocks, side), jnp.float32)
+    for first in range(0, slots, PACK):
+        total = total + dot(blocks_used(first, PACK, cols_ref, col_blocks, hot_cols), tiles, first)
     for k in range(col_blocks):
         at = k % NB_DEV * side
-        sums_ref[n_mem + k // NB_DEV, :, at : at + side] = col_total[k : k + 1]
+        sums_ref[n_mem + k // NB_DEV, :, at : at + side] = total[k : k + 1]
+    from_c = over_clu(0, lambda o: sums_ref.at[n_mem + o], lambda k: deg_c.at[k], deg_c)
 
     def turn(g, carry):
         for slot in [g * GROUP + k for k in range(GROUP)]:
@@ -288,10 +284,6 @@
     def row_sums():
         return place_sums(from_cols, turned, cols_ref, col_blocks, rows_ref, row_blocks)
 
-    pl.semaphore_wait(barrier, n_mem + n_clu - 2)
-
-    from_m = over_mem(0, lambda o: sums_ref.at[o], lambda k: deg_m.at[k], deg_m)
-    from_c = over_clu(0, lambda o: sums_ref.at[n_mem + o], lambda k: deg_c.at[k], deg_c)
     lax.fori_loop(0, steps // 2, turn, 0)
     degree = 1.0 + (sums_ref[me_m] + sums_ref[n_mem + me_c])
     from_m.wait()

time: 33.6 us -> 33.4 us (level)
  no operation moved by 1% of the time
where the time goes in v8:
time: 33.4 us; the launch traced here: 33.2 us
  Pallas kernels  31.9 us (96%)
  between operations  1.29 us (4%)
    pallas_call x1, Pallas kernels, on_device_kernel(): pl.pallas_call(functools.partial(solve_kernel, n_clu, n_mem), out_shape=r...  30.3 us
    pallas_call x1, Pallas kernels, on_device_kernel(): pl.pallas_call(finish_kernel, out_shape=results, in_specs=[hbm, hbm], out...  1.62 us

profile of v8, /device:TPU:0, one launch (start us, length us, event | category | flops | bytes accessed | tf_op | source)
XLA Modules:
  0.0 33.2 jit_solution(2489102283799403655)
XLA Ops:
  1.3 30.3 %solve.1 = (f32[8,256]{1,0:T(8,128)}, f32[8,256]{1,0:T(8,128)}) custom-call(s32[1,256]{1,0:T(1,128)} %bitcast.2, f32[1,256]{1,0:T(1,128)} %bitcast.3, bf16[1,1,96,128,128]{4,3,2,1,0:T(8,128)(2,1)} %tiles_hbm.1, s32[1,1,96]{2,1,0:T(1,128)} %rows_hbm.1, s32[1,1,96]{2,1,0:T(1,128)} %cols_hbm.1, s32[1,1]{1,0:T(1,128)S(6)} %copy.8.count_hbm), custom_call_target="tpu_custom_call" | custom-call | tf_op jit(solution)/shard_map/solve/pallas_call | solution.py:434
  31.6 1.6 %finish.1 = (f32[8,256]{1,0:T(8,128)}, f32[8,256]{1,0:T(8,128)}) custom-call(f32[8,256]{1,0:T(8,128)} %get-tuple-element.4.scores_in, f32[8,256]{1,0:T(8,128)} %get-tuple-element.5.residual_in), custom_call_target="tpu_custom_call" | custom-call | tf_op jit(solution)/shard_map/finish/pallas_call | solution.py:476

commit v9 on v8

--- a/solution.py
+++ b/solution.py
@@ -105,6 +105,8 @@
     rows_hbm,
     cols_hbm,
     count_hbm,
+    scores_hbm,
+    residual_hbm,
     scores_ref,
     residual_ref,
     class_ref,
@@ -112,6 +114,7 @@
     rows_ref,
     cols_ref,
     count_ref,
+    places,
     tiles,
     turned,
     hot_rows,
@@ -132,6 +135,7 @@
     dots_m,
     dots_c,
     load_sems,
+    out_sems,
     tile_sems,
     send_m,
     recv_m,
@@ -227,18 +231,26 @@
             preferred_element_type=jnp.float32,
         )
 
-    def blocks_used(first, count, own_ref, own_blocks, hot):
-        return [
-            hot[used(slot, own_ref[0, 0, slot], own_blocks)].astype(jnp.bfloat16)
-            for slot in range(first, first + count)
-        ]
+    def blocks_used(first, count, own_ref, own_blocks, hot, side_at, to_ref, to_blocks):
+        blocks = []
+        for slot in range(first, first + count):
+            block = used(slot, own_ref[0, 0, slot], own_blocks)
+            start = to_blocks - 1 - to_ref[0, 0, slot]
+            places[side_at, slot] = block * (2 * to_blocks - 1) + start
+            blocks.append(hot[block].astype(jnp.bfloat16))
+        return blocks
 
     total = jnp.zeros((row_blocks, side), jnp.float32)
     for g in range(steps):
         tile_copy(g).wait()
         for first in range(g * GROUP, (g + 1) * GROUP, 2):
             pair = lax.dot_general(
-                jnp.concatenate(blocks_used(first, 2, rows_ref, row_blocks, hot_rows), axis=0),
+                jnp.concatenate(
+                    blocks_used(
+                        first, 2, rows_ref, row_blocks, hot_rows, 0, cols_ref, col_blocks
+                    ),
+                    axis=0,
+                ),
                 tiles[pl.ds(first, 2)].reshape(2 * side, side),
                 (((1,), (1,)), ((), ())),
                 preferred_element_type=jnp.float32,
@@ -252,7 +264,10 @@
 
     total = jnp.zeros((col_blocks, side), jnp.float32)
     for first in range(0, slots, PACK):
-        total = total + dot(blocks_used(first, PACK, cols_ref, col_blocks, hot_cols), tiles, first)
+        left = blocks_used(
+            first, PACK, cols_ref, col_blocks, hot_cols, 1, rows_ref, row_blocks
+        )
+        total = total + dot(left, tiles, first)
     for k in range(col_blocks):
         at = k % NB_DEV * side
         sums_ref[n_mem + k // NB_DEV, :, at : at + side] = total[k : k + 1]
@@ -263,14 +278,12 @@
             turned[slot] = tiles[slot].T
         return carry
 
-    def place_sums(table, held, own_ref, own_blocks, to_ref, to_blocks):
+    def place_sums(table, held, side_at, to_blocks):
         def step(g, total):
             for k in range(0, SPAN, PACK):
                 left = []
                 for slot in [g * SPAN + k + e for e in range(PACK)]:
-                    block = used(slot, own_ref[0, 0, slot], own_blocks)
-                    start = to_blocks - 1 - to_ref[0, 0, slot]
-                    panel = table[block, pl.ds(start, to_blocks)]
+                    panel = table[pl.ds(places[side_at, slot], to_blocks)]
                     left.append(panel.reshape(to_blocks * CLASSES, side).astype(jnp.bfloat16))
                 total = total + dot(left, held, g * SPAN + k)
             return total
@@ -279,10 +292,10 @@
         return lax.fori_loop(0, slots // SPAN, step, zero)
 
     def column_sums():
-        return place_sums(from_rows, tiles, rows_ref, row_blocks, cols_ref, col_blocks)
+        return place_sums(from_rows, tiles, 0, col_blocks)
 
     def row_sums():
-        return place_sums(from_cols, turned, cols_ref, col_blocks, rows_ref, row_blocks)
+        return place_sums(from_cols, turned, 1, row_blocks)
 
     lax.fori_loop(0, steps // 2, turn, 0)
     degree = 1.0 + (sums_ref[me_m] + sums_ref[n_mem + me_c])
@@ -305,13 +318,13 @@
         from_c = over_clu(1 + 2 * step, lambda o: own.at[step], lambda k: pan_c.at[step, me_c], pan_c.at[step])
         return from_m, from_c
 
-    def place_panels(panels, count, table, at):
+    def place_panels(panels, count, table, to_blocks):
         blocks = []
         for k in range(count):
             panel = panels[k].astype(jnp.float32).reshape(NB_DEV, CLASSES, side)
             for e in range(NB_DEV):
                 blocks.append(panel[e])
-                table[k * NB_DEV + e, at] = panel[e]
+                table[(k * NB_DEV + e) * (2 * to_blocks - 1) + to_blocks - 1] = panel[e]
         return blocks
 
     def parts_of(out, parts, blocks):
@@ -322,14 +335,14 @@
     def multiply(step, from_m, from_c, between):
         phase = 2 + 2 * step
         from_c.wait()
-        place_panels(pan_c.at[step], n_clu, from_cols, row_blocks - 1)
+        place_panels(pan_c.at[step], n_clu, from_cols, row_blocks)
         out = row_sums()
         parts_of(out, part_m.at[step], row_blocks)
         back_m = over_mem(
             phase, lambda o: part_m.at[step, o], lambda k: got_m.at[step, k], got_m.at[step]
         )
         from_m.wait()
-        between(place_panels(pan_m.at[step], n_mem, from_rows, col_blocks - 1), out)
+        between(place_panels(pan_m.at[step], n_mem, from_rows, col_blocks), out)
         parts_of(column_sums(), part_c.at[step], col_blocks)
         back_c = over_clu(
             phase, lambda o: part_c.at[step, o], lambda k: got_c.at[step, k], got_c.at[step]
@@ -402,7 +415,13 @@
     scores_ref[...] = alpha * labels + alpha_next * direction
     residual_ref[...] = alpha * (first - ratio * labels) - alpha_next * image
 
-    for copy in sent:
+    results = [
+        pltpu.make_async_copy(scores_ref, scores_hbm, out_sems.at[0]),
+        pltpu.make_async_copy(residual_ref, residual_hbm, out_sems.at[1]),
+    ]
+    for copy in results:
+        copy.start()
+    for copy in sent + results:
         copy.wait()
 
 
@@ -426,7 +445,6 @@
     col_blocks = NB_DEV * n_clu
     f32 = jnp.float32
     hbm = pl.BlockSpec(memory_space=pltpu.HBM)
-    vmem = pl.BlockSpec(memory_space=pltpu.VMEM)
     dma = pltpu.SemaphoreType.DMA
     panel = (CLASSES, nodes)
     sent = (NB_DEV * CLASSES, side)
@@ -435,19 +453,22 @@
         functools.partial(solve_kernel, n_clu, n_mem),
         out_shape=results,
         in_specs=[hbm] * 6,
-        out_specs=(vmem, vmem),
+        out_specs=(hbm, hbm),
         scratch_shapes=[
+            pltpu.VMEM(panel, f32),
+            pltpu.VMEM(panel, f32),
             pltpu.VMEM((1, nodes), jnp.int32),
             pltpu.VMEM((1, nodes), f32),
             pltpu.SMEM(tile_rows.shape, jnp.int32),
             pltpu.SMEM(tile_cols.shape, jnp.int32),
             pltpu.SMEM(tile_count.shape, jnp.int32),
+            pltpu.SMEM((2, slots), jnp.int32),
             pltpu.VMEM((slots, side, side), tile_values.dtype),
             pltpu.VMEM((slots, side, side), tile_values.dtype),
             pltpu.VMEM((row_blocks + 1, row_blocks, side), f32),
             pltpu.VMEM((col_blocks + 1, col_blocks, side), f32),
-            pltpu.VMEM((row_blocks + 1, 2 * col_blocks - 1, CLASSES, side), f32),
-            pltpu.VMEM((col_blocks + 1, 2 * row_blocks - 1, CLASSES, side), f32),
+            pltpu.VMEM(((row_blocks + 1) * (2 * col_blocks - 1), CLASSES, side), f32),
+            pltpu.VMEM(((col_blocks + 1) * (2 * row_blocks - 1), CLASSES, side), f32),
             pltpu.VMEM((n_mem + n_clu, 1, nodes), f32),
             pltpu.VMEM((n_mem, 1, nodes), f32),
             pltpu.VMEM((n_clu, 1, nodes), f32),
@@ -462,6 +483,7 @@
             pltpu.VMEM((n_mem, 1, 128), f32),
             pltpu.VMEM((n_clu, 1, 128), f32),
             dma((5,)),
+            dma((2,)),
             dma((slots // GROUP,)),
             dma((2 + 2 * ITERS,)),
             dma((2 + 2 * ITERS,)),

time: 33.4 us -> 33.4 us (level)
  no operation moved by 1% of the time
where the time goes in v9:
time: 33.4 us; the launch traced here: 33.2 us
  Pallas kernels  31.9 us (96%)
  between operations  1.29 us (4%)
    pallas_call x1, Pallas kernels, on_device_kernel(): pl.pallas_call(functools.partial(solve_kernel, n_clu, n_mem), out_shape=r...  30.3 us
    pallas_call x1, Pallas kernels, on_device_kernel(): pl.pallas_call(finish_kernel, out_shape=results, in_specs=[hbm, hbm], out...  1.62 us

profile of v9, /device:TPU:0, one launch (start us, length us, event | category | flops | bytes accessed | tf_op | source)
XLA Modules:
  0.0 33.2 jit_solution(10477257931410558654)
XLA Ops:
  1.3 30.3 %solve.1 = (f32[8,256]{1,0:T(8,128)}, f32[8,256]{1,0:T(8,128)}) custom-call(s32[1,256]{1,0:T(1,128)} %bitcast.2, f32[1,256]{1,0:T(1,128)} %bitcast.3, bf16[1,1,96,128,128]{4,3,2,1,0:T(8,128)(2,1)} %tiles_hbm.1, s32[1,1,96]{2,1,0:T(1,128)} %rows_hbm.1, s32[1,1,96]{2,1,0:T(1,128)} %cols_hbm.1, s32[1,1]{1,0:T(1,128)S(6)} %copy.8.count_hbm), custom_call_target="tpu_custom_call" | custom-call | tf_op jit(solution)/shard_map/solve/pallas_call | solution.py:452
  31.6 1.6 %finish.1 = (f32[8,256]{1,0:T(8,128)}, f32[8,256]{1,0:T(8,128)}) custom-call(f32[8,256]{1,0:T(8,128)} %get-tuple-element.4.scores_in, f32[8,256]{1,0:T(8,128)} %get-tuple-element.5.residual_in), custom_call_target="tpu_custom_call" | custom-call | tf_op jit(solution)/shard_map/finish/pallas_call | solution.py:498
